TPU v7x, 32 devices: a whole 2x2x4 slice. The times are simulated.
32 devices in a mesh: slab: 8 (over y, x, core), pencil: 4 (over z).
Axes of the slice: x: 2, y: 2, z: 4, core: 2. Of those that a mesh axis runs over, the one named last changes fastest.
Arguments:
- orbitals: float32 [4, 192, 192, 192], P(None, 'slab', 'pencil'), may hold values from -6 to 6
- potential: float32 [192, 192, 192], P('slab', 'pencil'), may hold values from 0.5 to 2.5
- unlocked: int32 [4], replicated, may hold values 0 or 1
Outputs:
- orthonormal: float32 [4, 192, 192, 192], P(None, 'slab', 'pencil')
Inputs may be any that keep to these rules, and one draw needn't show every extreme that they name: `unlocked`: 1 marks a band that is filtered, 0 a locked band kept as it is.
All inputs are finite; a program needn't handle non-finite values.
Results may differ from a plain program's by a relative error of at most 0.00005.
Values sent between devices are 32-bit elements; how exact they have to be, the bound alone decides.
A program may use at most 128 MiB of HBM per device.

v0:
```python
import math

import jax
import jax.numpy as jnp
from jax import lax
from jax.sharding import PartitionSpec as P

NG = 192


kinetic_scale = 4.0
filter_center = 1.0
filter_half = 1.5
highest = lax.Precision.HIGHEST


def frequencies(number, length):
    index = jnp.arange(number, dtype=jnp.int32)
    if number == length:
        return jnp.where(index < length // 2, index, index - length)
    return index - length // 4


def tables(number, length):
    modes = frequencies(number, length)
    places = jnp.arange(length, dtype=jnp.int32)
    product = places[:, None] * modes[None, :] % length
    angle = 2.0 * math.pi / length * product.astype(jnp.float32)
    return (jnp.cos(angle), jnp.sin(angle))


def forward_table(cosine, sine):
    return jnp.stack([jnp.stack([cosine, -sine], 1), jnp.stack([sine, cosine], 1)], 1)


def inverse_table(cosine, sine):
    cos_t = cosine.T
    sin_t = sine.T
    return jnp.stack([jnp.stack([cos_t, sin_t], 1), jnp.stack([-sin_t, cos_t], 1)], 1)


def local(orbitals, potential, unlocked):
    length = orbitals.shape[3]
    kept_modes = length // 2
    cos_k, sin_k = tables(kept_modes, length)
    cos_f, sin_f = tables(length, length)
    first_forward = jnp.stack([cos_k, -sin_k], 1)
    first_inverse = jnp.stack([cos_k.T, -sin_k.T], 1)
    second_forward = forward_table(cos_k, sin_k)
    second_inverse = inverse_table(cos_k, sin_k)
    depth_forward = forward_table(cos_f, sin_f)
    depth_inverse = inverse_table(cos_f, sin_f)
    pencil_block = kept_modes // lax.axis_size("pencil")
    slab_block = kept_modes // lax.axis_size("slab")
    kept_list = frequencies(kept_modes, length)
    third_modes = lax.dynamic_slice_in_dim(
        kept_list, lax.axis_index("pencil") * pencil_block, pencil_block
    ).astype(jnp.float32)
    second_modes = lax.dynamic_slice_in_dim(
        kept_list, lax.axis_index("slab") * slab_block, slab_block
    ).astype(jnp.float32)
    first_modes = frequencies(length, length).astype(jnp.float32)
    squared = (
        third_modes[:, None, None] ** 2
        + second_modes[None, :, None] ** 2
        + first_modes[None, None, :] ** 2
    )
    radius = float((length // 4) ** 2)
    kinetic = jnp.where(squared < radius, kinetic_scale * squared / radius, 0.0)
    lines_k = jnp.einsum("bacx,xrk->bacrk", orbitals, first_forward, precision=highest)
    along_f = jnp.einsum(
        "bacrk,crsf->baksf",
        lax.all_to_all(lines_k, "pencil", split_axis=4, concat_axis=2, tiled=True),
        second_forward,
        precision=highest,
    )
    spectra = jnp.einsum(
        "baksf,astg->bkftg",
        lax.all_to_all(along_f, "slab", split_axis=4, concat_axis=1, tiled=True),
        depth_forward,
        precision=highest,
    )
    spectra = spectra * kinetic[None, :, :, None, :]
    along_a = jnp.einsum("bkftg,gtsa->bkfsa", spectra, depth_inverse, precision=highest)
    returned = lax.all_to_all(along_a, "slab", split_axis=4, concat_axis=2, tiled=True)
    rows_c = jnp.einsum("bkfsa,fsrc->bkarc", returned, second_inverse, precision=highest)
    lines_x = lax.all_to_all(rows_c, "pencil", split_axis=4, concat_axis=1, tiled=True)
    kinetic_part = jnp.einsum("bkarc,krx->bacx", lines_x, first_inverse, precision=highest)
    kinetic_part = kinetic_part / float(NG**3)
    applied = kinetic_part + potential[None] * orbitals
    filtered = jnp.where(
        unlocked[:, None, None, None] == 1,
        (applied - filter_center * orbitals) / filter_half,
        orbitals,
    )
    number = filtered.shape[0]
    flattened = filtered.reshape(number, -1)
    partial_intersection = jnp.dot(flattened, flattened.T, precision=highest) / float(NG**3)
    intersection = lax.psum(partial_intersection, ("slab", "pencil"))
    factor = jnp.linalg.cholesky(intersection)
    result = jax.scipy.linalg.solve_triangular(factor, flattened, lower=True)
    return result.reshape(filtered.shape)


def solution(mesh):
    in_specs = (P(None, "slab", "pencil", None), P("slab", "pencil", None), P())
    out_specs = P(None, "slab", "pencil", None)
    return jax.shard_map(local, mesh=mesh, in_specs=in_specs, out_specs=out_specs, check_vma=False)
```

profile of v0, /device:TPU:0, one launch (start us, length us, event | category | flops | bytes accessed | tf_op | source)
XLA Modules:
  0.0 789.0 jit_solution(7045103650904252148)
XLA Ops:
  1.8 8.4 %fusion.18 = f32[4,24,48,2,96]{4,2,1,0,3:T(8,128)} fusion(f32[4,24,48,192]{3,2,1,0:T(8,128)} %param.3, f32[192,1,96]{2,0,1:T(8,128)S(1)} %get-tuple-element.23, f32[192,1,96]{2,0,1:T(8,128)S(1)} %get-tuple-element.24), kind=kOutput, calls=%fused_computation.20 | convolution fusion | flops 2038468608 | bytes 7225344 | tf_op jit(solution)/shard_map/bacx,xrk->bacrk/dot_general | solution.py:70
  10.1 10.5 %copy.34 = f32[4,24,48,2,96]{2,1,0,3,4:T(8,128)} copy(f32[4,24,48,2,96]{4,2,1,0,3:T(8,128)} %fusion.18) | data formatting | bytes 7077888 | tf_op jit(solution)/shard_map/bacx,xrk->bacrk/dot_general | solution.py:70
  20.6 11.5 %reshape.515 = f32[4,1,221184]{2,1,0:T(1,128)} reshape(f32[96,2,4,24,48]{4,3,2,1,0:T(8,128)} %bitcast.163) | data formatting | bytes 7077888
  32.0 6.8 all-to-all-start
  40.6 77.3 %all-to-all-done = f32[4,1,221184]{2,1,0:T(1,128)S(1)} async-done(((f32[4,1,221184]{2,1,0:T(1,128)}), f32[4,1,221184]{2,1,0:T(1,128)S(1)}, u32[]{:S(2)}, u32[]{:S(2)}) %all-to-all-start) | async-done | bytes 3538976 | tf_op jit(solution)/shard_map/all_to_all | solution.py:73
  118.4 32.6 %reduce.6 = f32[4,221184]{1,0:T(4,128)} reduce(f32[4,1,221184]{2,1,0:T(1,128)S(1)} %all-to-all-done, f32[]{:T(128)} %broadcast.675), dimensions={1}, to_apply=%all_to_all.52.reduce_sub_computation | reduce | bytes 7077892 | tf_op jit(solution)/shard_map/all_to_all | solution.py:73
  151.1 10.0 %reshape.516 = f32[96,2,4,24,48]{4,3,2,1,0:T(8,128)} reshape(f32[4,221184]{1,0:T(4,128)} %reduce.6) | data formatting | bytes 7077888
  161.1 13.4 %copy.36 = f32[4,24,4,48,2,24]{3,2,5,4,1,0:T(4,128)} copy(f32[4,24,4,48,2,24]{3,1,0,4,5,2:T(8,128)} %bitcast.164) | data formatting | bytes 7077888 | tf_op jit(solution)/shard_map/all_to_all | solution.py:73
  174.5 9.5 %reshape.496 = f32[4,24,192,2,24,1]{2,4,3,1,0,5:T(8,128)} reshape(f32[4,24,4,48,2,24]{3,2,5,4,1,0:T(4,128)} %copy.36) | data formatting | bytes 7077888 | tf_op jit(solution)/shard_map/all_to_all | solution.py:73
  184.0 6.4 fusion.27
  190.4 9.3 %copy.38 = f32[4,24,24,2,96]{2,3,1,0,4:T(2,128)} copy(f32[4,24,24,2,96]{4,2,3,1,0:T(8,128)S(1)} %fusion.27) | data formatting | bytes 3538944 | tf_op jit(solution)/shard_map/bacrk,crsf->baksf/dot_general | solution.py:71
  199.7 18.5 %reshape.517 = f32[8,1,55296]{2,1,0:T(1,128)} reshape(f32[96,4,24,2,24]{4,3,2,1,0:T(2,128)} %bitcast.165) | data formatting | bytes 3538944
  226.6 18.5 %all-to-all-done.1 = f32[8,1,55296]{2,1,0:T(1,128)S(1)} async-done(((f32[8,1,55296]{2,1,0:T(1,128)}), f32[8,1,55296]{2,1,0:T(1,128)S(1)}, u32[]{:S(2)}, u32[]{:S(2)}) %all-to-all-start.1) | async-done | bytes 1769504 | tf_op jit(solution)/shard_map/all_to_all | solution.py:79
  249.9 19.4 %reshape.518 = f32[96,4,24,2,24]{4,3,2,1,0:T(2,128)} reshape(f32[8,55296]{1,0:T(8,128)S(1)} %reduce.7) | data formatting | bytes 3538944
  269.3 7.9 %copy.39 = f32[4,24,24,2,96]{2,1,4,3,0:T(8,128)} copy(f32[4,24,24,2,96]{2,3,1,0,4:T(2,128)} %bitcast.166) | data formatting | bytes 3538944 | tf_op jit(solution)/shard_map/all_to_all | solution.py:79
  277.3 9.6 %copy.78 = f32[4,8,24,24,2,12]{2,1,3,4,5,0:T(8,128)} copy(f32[4,8,24,24,2,12]{3,2,5,1,4,0:T(8,128)} %bitcast.167) | data formatting | bytes 3538944 | tf_op jit(solution)/shard_map/all_to_all | solution.py:79
  301.2 9.5 %copy.44 = f32[4,24,12,2,192]{1,3,2,0,4:T(2,128)} copy(f32[4,24,12,2,192]{4,1,3,2,0:T(8,128)S(1)} %fusion.24) | data formatting | bytes 3538944 | tf_op jit(solution)/shard_map/bkftg,gtsa->bkfsa/dot_general | solution.py:84
  310.7 18.5 %reshape.519 = f32[8,1,55296]{2,1,0:T(1,128)} reshape(f32[192,4,12,2,24]{4,3,2,1,0:T(2,128)} %bitcast.168) | data formatting | bytes 3538944
  334.9 20.9 %all-to-all-done.2 = f32[8,1,55296]{2,1,0:T(1,128)S(1)} async-done(((f32[8,1,55296]{2,1,0:T(1,128)}), f32[8,1,55296]{2,1,0:T(1,128)S(1)}, u32[]{:S(2)}, u32[]{:S(2)}) %all-to-all-start.2) | async-done | bytes 1769504 | tf_op jit(solution)/shard_map/all_to_all | solution.py:85
  360.7 19.4 %reshape.520 = f32[192,4,12,2,24]{4,3,2,1,0:T(2,128)} reshape(f32[8,55296]{1,0:T(8,128)S(1)} %reduce.8) | data formatting | bytes 3538944
  380.1 13.9 %copy.45 = f32[4,24,12,2,8,24]{5,1,3,2,4,0:T(8,128)} copy(f32[4,24,12,2,8,24]{1,3,2,0,5,4:T(2,128)} %bitcast.169) | data formatting | bytes 3538944 | tf_op jit(solution)/shard_map/all_to_all | solution.py:85
  394.0 21.7 %fusion.21 = f32[4,24,24,2,192]{4,2,3,1,0:T(8,128)} fusion(f32[4,24,96,2,24,1]{4,1,3,2,0,5:T(8,128)} %bitcast.161, f32[96,1,2,192]{3,0,1,2:T(8,128)S(1)} %copy-done.14, f32[96,1,2,192]{3,0,1,2:T(8,128)S(1)} %copy-done.13), kind=kOutput, calls=%fused_computation.21 | convolution fusion | flops 2038505472 | bytes 5603328 | tf_op jit(solution)/shard_map/bkfsa,fsrc->bkarc/dot_general | solution.py:86
  415.8 23.2 %copy.48 = f32[4,24,24,2,192]{2,3,1,0,4:T(2,128)} copy(f32[4,24,24,2,192]{4,2,3,1,0:T(8,128)} %fusion.21) | data formatting | bytes 7077888 | tf_op jit(solution)/shard_map/bkfsa,fsrc->bkarc/dot_general | solution.py:86
  438.9 46.5 %reshape.521 = f32[4,1,221184]{2,1,0:T(1,128)} reshape(f32[192,4,24,2,24]{4,3,2,1,0:T(2,128)} %bitcast.159) | data formatting | bytes 7077888
  489.3 76.5 %all-to-all-done.3 = f32[4,1,221184]{2,1,0:T(1,128)S(1)} async-done(((f32[4,1,221184]{2,1,0:T(1,128)}), f32[4,1,221184]{2,1,0:T(1,128)S(1)}, u32[]{:S(2)}, u32[]{:S(2)}) %all-to-all-start.3) | async-done | bytes 3538976 | tf_op jit(solution)/shard_map/all_to_all | solution.py:87
  565.8 32.8 %reduce.9 = f32[4,221184]{1,0:T(4,128)} reduce(f32[4,1,221184]{2,1,0:T(1,128)S(1)} %all-to-all-done.3, f32[]{:T(128)} %broadcast.675), dimensions={1}, to_apply=%all_to_all.64.reduce_sub_computation | reduce | bytes 7077892 | tf_op jit(solution)/shard_map/all_to_all | solution.py:87
  598.6 46.3 %reshape.522 = f32[192,4,24,2,24]{4,3,2,1,0:T(2,128)} reshape(f32[4,221184]{1,0:T(4,128)} %reduce.9) | data formatting | bytes 7077888
  644.9 32.7 %copy.85 = f32[4,24,24,2,4,48]{5,1,4,3,2,0:T(8,128)} copy(f32[4,24,24,2,4,48]{2,3,1,0,5,4:T(2,128)} %bitcast.160) | data formatting | bytes 7077888 | tf_op jit(solution)/shard_map/all_to_all | solution.py:87
  677.5 19.6 %fusion.7 = f32[4,24,48,192]{3,2,1,0:T(8,128)S(1)} fusion(f32[4,24,48,192]{3,2,1,0:T(8,128)} %param.3, f32[24,48,192]{2,1,0:T(8,128)S(1)} %copy-done.1, pred[4]{0:T(512)(128)(4,1)S(1)} %broadcast_compare_fusion, f32[4,96,24,2,48]{4,1,3,2,0:T(8,128)} %bitcast.162, f32[96,1,192]{2,0,1:T(8,128)S(1)} %copy-done.10, f32[96,1,192]{2,0,1:T(8,128)S(1)} %copy-done.8), kind=kOutput, calls=%fused_computation.8 | convolution fusion | flops 2043777024 | bytes 11649028 | tf_op jit(solution)/shard_map/bkarc,krx->bacx/dot_general | solution.py:88
  699.4 20.3 %fusion.34 = f32[4,4]{0,1:T(4,128)S(1)} fusion(f32[4,24,48,192]{3,2,1,0:T(8,128)S(1)} %fusion.7), kind=kOutput, calls=%fused_computation.26 | convolution fusion | flops 42467344 | bytes 3539008 | tf_op jit(solution)/shard_map/dot_general | solution.py:98
  724.8 38.9 %psum.7 = f32[4,4]{0,1:T(4,128)S(1)} all-reduce(f32[4,4]{0,1:T(4,128)S(1)} %fusion.34), channel_id=1, replica_groups=mesh['slab'=8,'pencil'=4] {'slab','pencil'}, use_global_device_ids=true, to_apply=%region_0.1 | all-reduce | flops 16 | bytes 128 | tf_op jit(solution)/shard_map/psum | solution.py:99
  770.7 15.0 %fusion.10 = f32[4,24,48,192]{3,0,2,1:T(4,128)S(1)} fusion(f32[24,48,192,4]{2,1,0,3:T(8,128)} %triangular_solve.39, f32[1,4,4]{1,2,0:T(4,128)S(1)} %custom-call.7), kind=kOutput, calls=%fused_computation.11 | convolution fusion | flops 42467328 | bytes 7077952 | tf_op jit(solution)/shard_map/jit(_solve_triangular)/triangular_solve | solution.py:101
  (70 shorter events, 63.4 us)
Async XLA Ops:
  1.1 0.6 copy-start.11
  1.1 0.7 copy-start.12
  32.0 85.9 %all-to-all-start = ((f32[4,1,221184]{2,1,0:T(1,128)}), f32[4,1,221184]{2,1,0:T(1,128)S(1)}, u32[]{:S(2)}, u32[]{:S(2)}) async-start(f32[4,1,221184]{2,1,0:T(1,128)} %reshape.515), calls=%async_computation | async-start | bytes 7077888 | tf_op jit(solution)/shard_map/all_to_all | solution.py:73
  174.5 9.5 %copy-start.15 = (f32[192,1,2,96]{3,0,2,1:T(8,128)S(1)}, f32[192,1,2,96]{3,0,2,1:T(8,128)}, u32[]{:S(2)}) copy-start(f32[192,1,2,96]{3,0,2,1:T(8,128)} %get-tuple-element.11) | copy-start | bytes 442372
  174.5 9.5 %copy-start.16 = (f32[192,1,2,96]{3,0,2,1:T(8,128)S(1)}, f32[192,1,2,96]{3,0,2,1:T(8,128)}, u32[]{:S(2)}) copy-start(f32[192,1,2,96]{3,0,2,1:T(8,128)} %get-tuple-element.12) | copy-start | bytes 442372
  218.2 26.9 %all-to-all-start.1 = ((f32[8,1,55296]{2,1,0:T(1,128)}), f32[8,1,55296]{2,1,0:T(1,128)S(1)}, u32[]{:S(2)}, u32[]{:S(2)}) async-start(f32[8,1,55296]{2,1,0:T(1,128)} %reshape.517), calls=%async_computation.1 | async-start | bytes 3538944 | tf_op jit(solution)/shard_map/all_to_all | solution.py:79
  286.9 6.3 copy-start.4
  286.9 6.3 copy-start.5
  293.1 4.1 copy-start.2
  293.1 4.1 copy-start.3
  293.1 4.1 copy-start.6
  329.2 26.7 %all-to-all-start.2 = ((f32[8,1,55296]{2,1,0:T(1,128)}), f32[8,1,55296]{2,1,0:T(1,128)S(1)}, u32[]{:S(2)}, u32[]{:S(2)}) async-start(f32[8,1,55296]{2,1,0:T(1,128)} %reshape.519), calls=%async_computation.2 | async-start | bytes 3538944 | tf_op jit(solution)/shard_map/all_to_all | solution.py:85
  333.5 0.7 copy-start.7
  333.5 0.7 copy-start.9
  380.1 13.9 %copy-start.13 = (f32[96,1,2,192]{3,0,1,2:T(8,128)S(1)}, f32[96,1,2,192]{3,0,1,2:T(8,128)}, u32[]{:S(2)}) copy-start(f32[96,1,2,192]{3,0,1,2:T(8,128)} %get-tuple-element.9) | copy-start | bytes 442372
  380.1 13.9 %copy-start.14 = (f32[96,1,2,192]{3,0,1,2:T(8,128)S(1)}, f32[96,1,2,192]{3,0,1,2:T(8,128)}, u32[]{:S(2)}) copy-start(f32[96,1,2,192]{3,0,1,2:T(8,128)} %get-tuple-element.10) | copy-start | bytes 442372
  485.4 3.9 copy-start.17
  485.4 80.3 %all-to-all-start.3 = ((f32[4,1,221184]{2,1,0:T(1,128)}), f32[4,1,221184]{2,1,0:T(1,128)S(1)}, u32[]{:S(2)}, u32[]{:S(2)}) async-start(f32[4,1,221184]{2,1,0:T(1,128)} %reshape.521), calls=%async_computation.3 | async-start | bytes 7077888 | tf_op jit(solution)/shard_map/all_to_all | solution.py:87
  644.9 32.7 %copy-start.1 = (f32[24,48,192]{2,1,0:T(8,128)S(1)}, f32[24,48,192]{2,1,0:T(8,128)}, u32[]{:S(2)}) copy-start(f32[24,48,192]{2,1,0:T(8,128)} %param.4) | copy-start | bytes 2654212
  644.9 32.7 %copy-start.8 = (f32[96,1,192]{2,0,1:T(8,128)S(1)}, f32[96,1,192]{2,0,1:T(8,128)}, u32[]{:S(2)}) copy-start(f32[96,1,192]{2,0,1:T(8,128)} %copy-done.7) | copy-start | bytes 221188
  644.9 32.7 %copy-start.10 = (f32[96,1,192]{2,0,1:T(8,128)S(1)}, f32[96,1,192]{2,0,1:T(8,128)}, u32[]{:S(2)}) copy-start(f32[96,1,192]{2,0,1:T(8,128)} %copy-done.9) | copy-start | bytes 221188
  697.2 2.2 copy-start
where the time goes:
time: 799 us; the launch traced here: 789 us
  local copies, waits for them, and re-layouts  353 us (44%)
  waiting for transfers between devices  193 us (24%)
  matrix products  99.4 us (12%)
  other arithmetic  85.9 us (11%)
  blocking collectives  38.9 us (5%)
  starting transfers between devices  18.1 us (2%)
    unnamed x44, local copies, waits for them, and re-layouts  194 us
    all_to_all x1, waiting for transfers between devices, local(): lax.all_to_all(lines_k, 'pencil', split_axis=4, concat_axis=2, tiled=True)  77.3 us
    all_to_all x1, waiting for transfers between devices, local(): lax.all_to_all(rows_c, 'pencil', split_axis=4, concat_axis=1, tiled=True)  76.5 us
    psum x1, blocking collectives, local(): intersection = lax.psum(partial_intersection, ('slab', 'pencil'))  38.9 us
    all_to_all x1, other arithmetic, local(): lax.all_to_all(rows_c, 'pencil', split_axis=4, concat_axis=1, tiled=True)  32.8 us
    all_to_all x1, local copies, waits for them, and re-layouts, local(): lax.all_to_all(rows_c, 'pencil', split_axis=4, concat_axis=1, tiled=True)  32.7 us
    all_to_all x1, other arithmetic, local(): lax.all_to_all(lines_k, 'pencil', split_axis=4, concat_axis=2, tiled=True)  32.6 us
    all_to_all x3, local copies, waits for them, and re-layouts, local(): lax.all_to_all(along_f, 'slab', split_axis=4, concat_axis=1, tiled=True)  23.8 us
  transfers between devices with their start and end apart: 4, of which 4 were waited for; matrix products, arithmetic and copies ran while one was open for 1% of the time, Pallas kernels for 0%

commit v1 on v0

--- a/solution.py
+++ b/solution.py
@@ -1,9 +1,326 @@
+import functools
 import math
 
 import jax
 import jax.numpy as jnp
+import numpy as np
 from jax import lax
+from jax.experimental import pallas as pl
+from jax.experimental.pallas import tpu as pltpu
 from jax.sharding import PartitionSpec as P
+
+MESH = pl.DeviceIdType.MESH
+
+
+def dft_tables(length, slabs, pencils, chunks):
+    half = length // 4
+    pair = half // (slabs * chunks)
+    place = np.arange(length)
+    modes = np.arange(2 * half) - half
+    third = np.arange(half)
+
+    def waves(mode):
+        angle = 2.0 * np.pi / length * ((mode[:, None] * place[None, :]) % length)
+        return np.cos(angle), np.sin(angle)
+
+    cos_k, sin_k = waves(third)
+    weight = np.where(third == 0, 1.0, 2.0)[:, None]
+
+    def order(cosine, sine):
+        both = np.stack([cosine, sine], 0).reshape(2, chunks, slabs, pair, length)
+        return both.transpose(1, 2, 0, 3, 4).reshape(2 * half, length)
+
+    forward_x = order(cos_k, -sin_k)
+    inverse_x = order(weight * cos_k, -weight * sin_k)
+    cosine, sine = waves(modes)
+    forward = np.stack([np.stack([cosine, sine], 1), np.stack([-sine, cosine], 1)], 0)
+    inverse = np.stack([np.stack([cosine.T, -sine.T], 1), np.stack([sine.T, cosine.T], 1)], 0)
+    f_block = 2 * half // pencils
+    a_block = length // slabs
+    c_block = length // pencils
+    forward_a = forward.reshape(2, pencils, f_block, 2 * length).transpose(1, 0, 2, 3).reshape(4 * half, 2 * length)
+    forward_c = forward.reshape(4 * half, 2 * length).T
+    inverse_c = inverse.reshape(2, pencils, c_block, 4 * half).transpose(1, 0, 2, 3).reshape(2 * length, 4 * half).T
+    inverse_a = inverse.reshape(2, slabs, a_block, 4 * half).transpose(1, 0, 2, 3).reshape(2 * length, 4 * half)
+    tables = (forward_x, forward_a, forward_c, inverse_c, inverse_a, inverse_x)
+    return [np.ascontiguousarray(t, dtype=np.float32) for t in tables]
+
+
+def matmul(left, right, contract=((1,), (0,))):
+    return lax.dot_general(
+        left, right, (contract, ((), ())), precision=lax.Precision.HIGHEST, preferred_element_type=jnp.float32
+    )
+
+
+def kernel(sizes, unlocked, orbitals, potential, fx, fa, fc, ic, ia, ix, row_k, row_f, col_s, out,
+           lines, s1, r1, s2, r2, s3, r3, s4, r4, back, sums, g1, h1, g2, h2,
+           own, send1, recv1, send2, recv2, send3, recv3, send4, recv4, gs1, gr1, gs2, gr2):
+    slabs, pencils, chunks, pair, bands, length = sizes
+    rows_a = orbitals.shape[1]
+    rows_c = orbitals.shape[2]
+    half = length // 4
+    f_block = 2 * half // pencils
+    wide = bands * rows_c
+    i_s = lax.axis_index("slab")
+    i_p = lax.axis_index("pencil")
+
+    def slab_peer(d):
+        return lax.rem(i_s + d, slabs)
+
+    def pencil_peer(d):
+        return lax.rem(i_p + d, pencils)
+
+    barrier = pltpu.get_barrier_semaphore()
+    for d in range(1, slabs):
+        pl.semaphore_signal(barrier, inc=1, device_id=(slab_peer(d), i_p), device_id_type=MESH)
+    for d in range(1, pencils):
+        pl.semaphore_signal(barrier, inc=1, device_id=(i_s, pencil_peer(d)), device_id_type=MESH)
+
+    def to_slab(d, src, dst, send, recv):
+        return pltpu.make_async_remote_copy(
+            src_ref=src, dst_ref=dst, send_sem=send, recv_sem=recv,
+            device_id=(slab_peer(d), i_p), device_id_type=MESH)
+
+    def to_pencil(d, src, dst, send, recv):
+        return pltpu.make_async_remote_copy(
+            src_ref=src, dst_ref=dst, send_sem=send, recv_sem=recv,
+            device_id=(i_s, pencil_peer(d)), device_id_type=MESH)
+
+    mine_a = pl.ds(pl.multiple_of(i_s * rows_a, 8), rows_a)
+    mine_f = pl.ds(pl.multiple_of(i_p * f_block, 8), f_block)
+
+    def copies(which, q):
+        if which == 0:
+            remote = [to_slab(d, s1.at[q, slab_peer(d)], r1.at[q, :, mine_a, :], send1.at[q, d], recv1.at[q, d])
+                      for d in range(1, slabs)]
+            local = pltpu.make_async_copy(s1.at[q, i_s], r1.at[q, :, mine_a, :], own.at[0, q])
+        elif which == 1:
+            remote = [to_pencil(d, s2.at[q, pencil_peer(d)], r2.at[q, i_p], send2.at[q, d], recv2.at[q, d])
+                      for d in range(1, pencils)]
+            local = pltpu.make_async_copy(s2.at[q, i_p], r2.at[q, i_p], own.at[1, q])
+        elif which == 2:
+            remote = [to_pencil(d, s3.at[q, pencil_peer(d)], r3.at[q, :, mine_f, :], send3.at[q, d], recv3.at[q, d])
+                      for d in range(1, pencils)]
+            local = pltpu.make_async_copy(s3.at[q, i_p], r3.at[q, :, mine_f, :], own.at[2, q])
+        else:
+            remote = [to_slab(d, s4.at[q, slab_peer(d)], r4.at[q, i_s], send4.at[q, d], recv4.at[q, d])
+                      for d in range(1, slabs)]
+            local = pltpu.make_async_copy(s4.at[q, i_s], r4.at[q, i_s], own.at[3, q])
+        return remote, local
+
+    def start(which, q):
+        remote, local = copies(which, q)
+        for copy in remote:
+            copy.start()
+        local.start()
+
+    def arrived(which, q):
+        remote, local = copies(which, q)
+        for copy in remote:
+            copy.wait_recv()
+        local.wait()
+
+    modes_x = 2 * half
+
+    def forward_line(a, carry):
+        rows = orbitals[:, pl.ds(a, 1)].reshape(wide, length)
+        result = matmul(fx[...], rows, ((1,), (1,)))
+        at = pl.multiple_of(a * modes_x, modes_x)
+        for t in range(lines.shape[0]):
+            low, high = t * 128, min(t * 128 + 128, wide)
+            lines[t, pl.ds(at, modes_x), 0:high - low] = result[:, low:high]
+        return carry
+
+    lax.fori_loop(0, rows_a, forward_line, 0)
+    pl.semaphore_wait(barrier, slabs - 1 + pencils - 1)
+
+    def line_rows(ref, i):
+        parts = []
+        for t in range(ref.shape[0]):
+            size = min(128, wide - t * 128)
+            parts.append(ref[t, pl.ds(i, rows_a, stride=modes_x), :][:, :size])
+        return parts
+
+    for q in range(chunks):
+        for j in range(slabs):
+            for r in range(2):
+                parts = []
+                for k in range(pair):
+                    parts += line_rows(lines, ((q * slabs + j) * 2 + r) * pair + k)
+                s1[q, j, r] = jnp.concatenate(parts, 1)
+        start(0, q)
+
+    packed = pair * wide
+    for q in range(chunks):
+        arrived(0, q)
+        result = matmul(fa[...], r1[q].reshape(2 * length, packed))
+        s2[q] = result.reshape(pencils, 2, f_block, packed)
+        start(1, q)
+
+    for q in range(chunks):
+        arrived(1, q)
+        blocks = []
+        for kb in range(pair * bands):
+            lanes = slice(kb * rows_c, (kb + 1) * rows_c)
+            blocks.append(jnp.concatenate([r2[q, p, r, :, lanes] for r in range(2) for p in range(pencils)], 1))
+        spectrum = matmul(jnp.concatenate(blocks, 0), fc[...])
+        mode_k = row_k[...] + (q * slabs * pair + i_s * pair).astype(jnp.float32)
+        mode_f = row_f[...] + (i_p * f_block - half).astype(jnp.float32)
+        squared = mode_k * mode_k + mode_f * mode_f + col_s[...]
+        radius = float(half * half)
+        kinetic = jnp.where(squared < radius, 4.0 * squared / radius, 0.0) * (1.0 / float(length**3))
+        result = matmul(spectrum * kinetic, ic[...])
+        for p in range(pencils):
+            for r in range(2):
+                lanes = slice((p * 2 + r) * rows_c, (p * 2 + r + 1) * rows_c)
+                s3[q, p, r] = jnp.concatenate(
+                    [result[kb * f_block:(kb + 1) * f_block, lanes] for kb in range(pair * bands)], 1)
+        start(2, q)
+
+    for q in range(chunks):
+        arrived(2, q)
+        result = matmul(ia[...], r3[q].reshape(4 * half, packed))
+        s4[q] = result.reshape(slabs, 2, rows_a, packed)
+        start(3, q)
+
+    for q in range(chunks):
+        arrived(3, q)
+        for j in range(slabs):
+            for r in range(2):
+                value = r4[q, j, r]
+                for k in range(pair):
+                    i = ((q * slabs + j) * 2 + r) * pair + k
+                    for t in range(back.shape[0]):
+                        low, high = t * 128, min(t * 128 + 128, wide)
+                        piece = value[:, k * wide + low:k * wide + high]
+                        if high - low < 128:
+                            piece = jnp.concatenate([piece, jnp.zeros((rows_a, 128 - high + low), jnp.float32)], 1)
+                        back[t, pl.ds(i, rows_a, stride=modes_x), :] = piece
+
+    sums[...] = jnp.zeros_like(sums)
+
+    def inverse_line(a, carry):
+        at = pl.multiple_of(a * modes_x, modes_x)
+        spectrum = jnp.concatenate(
+            [back[t, pl.ds(at, modes_x), 0:min(128, wide - t * 128)] for t in range(back.shape[0])], 1)
+        kinetic_part = matmul(spectrum, ix[...], ((0,), (0,)))
+        level = potential[pl.ds(a, 1)].reshape(rows_c, length)
+        filtered = []
+        for b in range(bands):
+            orbital = orbitals[b, pl.ds(a, 1)].reshape(rows_c, length)
+            applied = kinetic_part[b * rows_c:(b + 1) * rows_c] + level * orbital
+            value = jnp.where(unlocked[b] == 1, (applied - orbital) / 1.5, orbital)
+            out[b, pl.ds(a, 1)] = value.reshape(1, rows_c, length)
+            filtered.append(value)
+        n = 0
+        for b in range(bands):
+            for e in range(b + 1):
+                product = filtered[b] * filtered[e]
+                sums[n] += product.reshape(rows_c // 8, 8, length).sum(0)
+                n += 1
+        return carry
+
+    lax.fori_loop(0, rows_a, inverse_line, 0)
+
+    total = jnp.sum(jnp.sum(sums[...], axis=1), axis=1, keepdims=True)
+    g1[...] = jnp.broadcast_to(total, g1.shape)
+    shares = [to_slab(d, g1, h1.at[i_s], gs1.at[d], gr1.at[d]) for d in range(1, slabs)]
+    for copy in shares:
+        copy.start()
+    h1[pl.ds(i_s, 1)] = g1[...][None]
+    for copy in shares:
+        copy.wait()
+    g2[...] = jnp.sum(h1[...], axis=0)
+    shares = [to_pencil(d, g2, h2.at[i_p], gs2.at[d], gr2.at[d]) for d in range(1, pencils)]
+    for copy in shares:
+        copy.start()
+    h2[pl.ds(i_p, 1)] = g2[...][None]
+    for copy in shares:
+        copy.wait()
+    gram = jnp.sum(h2[...], axis=0) / float(length**3)
+
+    factor = {}
+    for b in range(bands):
+        for e in range(b + 1):
+            n = b * (b + 1) // 2 + e
+            value = gram[n:n + 1, 0:1]
+            for m in range(e):
+                value = value - factor[b, m] * factor[e, m]
+            factor[b, e] = jnp.sqrt(value) if b == e else value / factor[e, e]
+    inverse = [1.0 / factor[b, b] for b in range(bands)]
+
+    def solve_line(a, carry):
+        solved = []
+        for b in range(bands):
+            value = out[b, pl.ds(a, 1)].reshape(rows_c, length)
+            for m in range(b):
+                value = value - factor[b, m] * solved[m]
+            value = value * inverse[b]
+            out[b, pl.ds(a, 1)] = value.reshape(1, rows_c, length)
+            solved.append(value)
+        return carry
+
+    lax.fori_loop(0, rows_a, solve_line, 0)
+    for which in range(4):
+        for q in range(chunks):
+            for copy in copies(which, q)[0]:
+                copy.wait_send()
+
+
+def by_kernel(slabs, pencils, chunks, orbitals, potential, unlocked):
+    bands, rows_a, rows_c, length = orbitals.shape
+    half = length // 4
+    pair = half // (slabs * chunks)
+    f_block = 2 * half // pencils
+    wide = bands * rows_c
+    packed = pair * wide
+    tiles = -(-wide // 128)
+    pairs = bands * (bands + 1) // 2
+    tables = dft_tables(length, slabs, pencils, chunks)
+    rows = np.arange(pair * bands * f_block)
+    row_k = (rows // (bands * f_block)).astype(np.float32)[:, None]
+    row_f = (rows % f_block).astype(np.float32)[:, None]
+    col_s = ((np.arange(4 * half) % (2 * half) - half).astype(np.float32) ** 2)[None, :]
+    vmem = pl.BlockSpec(memory_space=pltpu.VMEM)
+    f32 = jnp.float32
+    dma = pltpu.SemaphoreType.DMA
+    scratch = [
+        pltpu.VMEM((tiles, rows_a * 2 * half, 128), f32),
+        pltpu.VMEM((chunks, slabs, 2, rows_a, packed), f32),
+        pltpu.VMEM((chunks, 2, length, packed), f32),
+        pltpu.VMEM((chunks, pencils, 2, f_block, packed), f32),
+        pltpu.VMEM((chunks, pencils, 2, f_block, packed), f32),
+        pltpu.VMEM((chunks, pencils, 2, f_block, packed), f32),
+        pltpu.VMEM((chunks, 2, 2 * half, packed), f32),
+        pltpu.VMEM((chunks, slabs, 2, rows_a, packed), f32),
+        pltpu.VMEM((chunks, slabs, 2, rows_a, packed), f32),
+        pltpu.VMEM((tiles, rows_a * 2 * half, 128), f32),
+        pltpu.VMEM((pairs, 8, length), f32),
+        pltpu.VMEM((pairs, 128), f32),
+        pltpu.VMEM((slabs, pairs, 128), f32),
+        pltpu.VMEM((pairs, 128), f32),
+        pltpu.VMEM((pencils, pairs, 128), f32),
+        dma((4, chunks)),
+        dma((chunks, slabs)), dma((chunks, slabs)),
+        dma((chunks, pencils)), dma((chunks, pencils)),
+        dma((chunks, pencils)), dma((chunks, pencils)),
+        dma((chunks, slabs)), dma((chunks, slabs)),
+        dma((slabs,)), dma((slabs,)),
+        dma((pencils,)), dma((pencils,)),
+    ]
+    flops = 2 * rows_a * wide * length * 2 * half * 6
+    return pl.pallas_call(
+        functools.partial(kernel, (slabs, pencils, chunks, pair, bands, length)),
+        out_shape=jax.ShapeDtypeStruct(orbitals.shape, f32),
+        in_specs=[pl.BlockSpec(memory_space=pltpu.SMEM)] + [vmem] * 11,
+        out_specs=vmem,
+        scratch_shapes=scratch,
+        compiler_params=pltpu.CompilerParams(
+            collective_id=0, has_side_effects=True, vmem_limit_bytes=56 * 1024 * 1024),
+        cost_estimate=pl.CostEstimate(flops=flops, bytes_accessed=10 * 2**20, transcendentals=0),
+    )(unlocked, orbitals, potential, *[jnp.asarray(t) for t in tables],
+      jnp.asarray(row_k), jnp.asarray(row_f), jnp.asarray(col_s))
+
 
 NG = 192
 
@@ -39,7 +356,7 @@
     return jnp.stack([jnp.stack([cos_t, sin_t], 1), jnp.stack([-sin_t, cos_t], 1)], 1)
 
 
-def local(orbitals, potential, unlocked):
+def by_collectives(orbitals, potential, unlocked):
     length = orbitals.shape[3]
     kept_modes = length // 2
     cos_k, sin_k = tables(kept_modes, length)
@@ -103,6 +420,18 @@
 
 
 def solution(mesh):
+    slabs, pencils = mesh.shape["slab"], mesh.shape["pencil"]
+
+    def local(orbitals, potential, unlocked):
+        bands, rows_a, rows_c, length = orbitals.shape
+        half = length // 4
+        f_block = 2 * half // pencils
+        chunks = half // (2 * slabs)
+        fits = chunks > 0 and half % (2 * slabs) == 0 and rows_a % 8 == 0 and rows_c % 8 == 0 and f_block % 8 == 0
+        if fits:
+            return by_kernel(slabs, pencils, chunks, orbitals, potential, unlocked)
+        return by_collectives(orbitals, potential, unlocked)
+
     in_specs = (P(None, "slab", "pencil", None), P("slab", "pencil", None), P())
     out_specs = P(None, "slab", "pencil", None)
     return jax.shard_map(local, mesh=mesh, in_specs=in_specs, out_specs=out_specs, check_vma=False)

time: 799 us -> 105 us (0.13); the launches traced: 789 us -> 105 us
  local copies, waits for them, and re-layouts: 353 us -> 4.89 us
  waiting for transfers between devices: 193 us -> 0 us
  Pallas kernels: 0 us -> 100 us
  matrix products: 99.4 us -> 0 us
  other arithmetic: 85.9 us -> 0 us
  blocking collectives: 38.9 us -> 0 us
  starting transfers between devices: 18.1 us -> 0 us
    all_to_all x4 -> x0, waiting for transfers between devices: 193 us -> none  [the longest x1 77.3 us: local(): lax.all_to_all(lines_k, 'pencil', split_axis=4, concat_axis=2, tiled=True)]
    unnamed x44 -> x1, local copies, waits for them, and re-layouts: 194 us -> 4.89 us
    pallas_call x0 -> x1, Pallas kernels: none -> 100 us  [by_kernel(): pl.pallas_call(functools.partial(kernel, (slabs, pencils, chunks, pair, b...]
    all_to_all x8 -> x0, local copies, waits for them, and re-layouts: 93.7 us -> none  [the longest x1 32.7 us: local(): lax.all_to_all(rows_c, 'pencil', split_axis=4, concat_axis=1, tiled=True)]
    dot_general x7 -> x0, matrix products: 84.4 us -> none  [the longest x1 21.7 us: local(): jnp.einsum('bkfsa,fsrc->bkarc', returned, second_inverse, precision=highest)]
    all_to_all x4 -> x0, other arithmetic: 75.1 us -> none  [the longest x1 32.8 us: local(): lax.all_to_all(rows_c, 'pencil', split_axis=4, concat_axis=1, tiled=True)]
    dot_general x4 -> x0, local copies, waits for them, and re-layouts: 52.4 us -> none  [the longest x1 23.2 us: local(): jnp.einsum('bkfsa,fsrc->bkarc', returned, second_inverse, precision=highest)]
    psum x1 -> x0, blocking collectives: 38.9 us -> none  [local(): intersection = lax.psum(partial_intersection, ('slab', 'pencil'))]
  transfers between devices with their start and end apart: 4 -> 0, of which waited for: 4 -> 0; matrix products, arithmetic and copies ran while one was open for 1% -> 0% of each run, Pallas kernels for 0% -> 0%
where the time goes in v1:
time: 105 us
  Pallas kernels  100 us (95%)
  local copies, waits for them, and re-layouts  4.89 us (5%)
    pallas_call x1, Pallas kernels, by_kernel(): pl.pallas_call(functools.partial(kernel, (slabs, pencils, chunks, pair, b...  100 us
    unnamed x1, local copies, waits for them, and re-layouts  4.89 us

profile of v1, /device:TPU:0, one launch (start us, length us, event | category | flops | bytes accessed | tf_op | source)
XLA Modules:
  0.0 104.9 jit_solution(1449110607712188724)
XLA Ops:
  0.0 100.0 %shard_map.118 = f32[4,24,48,192]{3,2,1,0:T(8,128)} custom-call(s32[4]{0:T(128)} %unlocked.1, f32[4,24,48,192]{3,2,1,0:T(8,128)} %orbitals.1, f32[24,48,192]{2,1,0:T(8,128)} %potential.1, f32[96,192]{1,0:T(8,128)} %constant.18.clone.fx, f32[192,384]{1,0:T(8,128)} %constant.19.clone.fa, f32[384,192]{1,0:T(8,128)} %constant.20.clone.fc, ...), custom_call_target="tpu_custom_call" | custom-call | flops 1019215872 | bytes 10485760 | tf_op jit(solution)/shard_map/pallas_call | solution.py:312
  100.0 4.9 %copy.14 = f32[4,24,48,192]{3,2,1,0:T(8,128)} copy(f32[4,24,48,192]{3,2,1,0:T(8,128)} %shard_map.118) | data formatting | bytes 7077888

commit v2 on v1

--- a/solution.py
+++ b/solution.py
@@ -3,6 +3,7 @@
 
 import jax
 import jax.numpy as jnp
+import ml_dtypes
 import numpy as np
 from jax import lax
 from jax.experimental import pallas as pl
@@ -30,7 +31,7 @@
         both = np.stack([cosine, sine], 0).reshape(2, chunks, slabs, pair, length)
         return both.transpose(1, 2, 0, 3, 4).reshape(2 * half, length)
 
-    forward_x = order(cos_k, -sin_k)
+    forward_x = order(cos_k, -sin_k).T
     inverse_x = order(weight * cos_k, -weight * sin_k)
     cosine, sine = waves(modes)
     forward = np.stack([np.stack([cosine, sine], 1), np.stack([-sine, cosine], 1)], 0)
@@ -43,13 +44,31 @@
     inverse_c = inverse.reshape(2, pencils, c_block, 4 * half).transpose(1, 0, 2, 3).reshape(2 * length, 4 * half).T
     inverse_a = inverse.reshape(2, slabs, a_block, 4 * half).transpose(1, 0, 2, 3).reshape(2 * length, 4 * half)
     tables = (forward_x, forward_a, forward_c, inverse_c, inverse_a, inverse_x)
-    return [np.ascontiguousarray(t, dtype=np.float32) for t in tables]
-
-
-def matmul(left, right, contract=((1,), (0,))):
-    return lax.dot_general(
-        left, right, (contract, ((), ())), precision=lax.Precision.HIGHEST, preferred_element_type=jnp.float32
-    )
+    pairs = []
+    for table in tables:
+        high = table.astype(ml_dtypes.bfloat16)
+        low = (table - high.astype(np.float64)).astype(ml_dtypes.bfloat16)
+        pairs.append(np.stack([high, low], 0))
+    return pairs
+
+
+def split(value):
+    high = value.astype(jnp.bfloat16)
+    return high, (value - high.astype(jnp.float32)).astype(jnp.bfloat16)
+
+
+def product(left, right):
+    return jnp.dot(left, right, preferred_element_type=jnp.float32)
+
+
+def from_left(table, value):
+    high, low = split(value)
+    return product(table[0], high) + (product(table[0], low) + product(table[1], high))
+
+
+def from_right(value, table):
+    high, low = split(value)
+    return product(high, table[0]) + (product(low, table[0]) + product(high, table[1]))
 
 
 def kernel(sizes, unlocked, orbitals, potential, fx, fa, fc, ic, ia, ix, row_k, row_f, col_s, out,
@@ -122,16 +141,21 @@
 
     modes_x = 2 * half
 
-    def forward_line(a, carry):
-        rows = orbitals[:, pl.ds(a, 1)].reshape(wide, length)
-        result = matmul(fx[...], rows, ((1,), (1,)))
-        at = pl.multiple_of(a * modes_x, modes_x)
-        for t in range(lines.shape[0]):
-            low, high = t * 128, min(t * 128 + 128, wide)
-            lines[t, pl.ds(at, modes_x), 0:high - low] = result[:, low:high]
+    group = 4
+
+    def forward_lines(g, carry):
+        rows = jnp.concatenate(
+            [orbitals[:, pl.ds(g * group + n, 1)].reshape(wide, length) for n in range(group)], 0)
+        result = from_right(rows, fx)
+        for n in range(group):
+            turned = result[n * wide:(n + 1) * wide].T
+            at = pl.multiple_of((g * group + n) * modes_x, modes_x)
+            for t in range(lines.shape[0]):
+                low, high = t * 128, min(t * 128 + 128, wide)
+                lines[t, pl.ds(at, modes_x), 0:high - low] = turned[:, low:high]
         return carry
 
-    lax.fori_loop(0, rows_a, forward_line, 0)
+    lax.fori_loop(0, rows_a // group, forward_lines, 0)
     pl.semaphore_wait(barrier, slabs - 1 + pencils - 1)
 
     def line_rows(ref, i):
@@ -151,25 +175,26 @@
         start(0, q)
 
     packed = pair * wide
-    for q in range(chunks):
+
+    def first_forward(q):
         arrived(0, q)
-        result = matmul(fa[...], r1[q].reshape(2 * length, packed))
+        result = from_left(fa, r1[q].reshape(2 * length, packed))
         s2[q] = result.reshape(pencils, 2, f_block, packed)
         start(1, q)
 
-    for q in range(chunks):
+    def second(q):
         arrived(1, q)
         blocks = []
         for kb in range(pair * bands):
             lanes = slice(kb * rows_c, (kb + 1) * rows_c)
             blocks.append(jnp.concatenate([r2[q, p, r, :, lanes] for r in range(2) for p in range(pencils)], 1))
-        spectrum = matmul(jnp.concatenate(blocks, 0), fc[...])
+        spectrum = from_right(jnp.concatenate(blocks, 0), fc)
         mode_k = row_k[...] + (q * slabs * pair + i_s * pair).astype(jnp.float32)
         mode_f = row_f[...] + (i_p * f_block - half).astype(jnp.float32)
         squared = mode_k * mode_k + mode_f * mode_f + col_s[...]
         radius = float(half * half)
         kinetic = jnp.where(squared < radius, 4.0 * squared / radius, 0.0) * (1.0 / float(length**3))
-        result = matmul(spectrum * kinetic, ic[...])
+        result = from_right(spectrum * kinetic, ic)
         for p in range(pencils):
             for r in range(2):
                 lanes = slice((p * 2 + r) * rows_c, (p * 2 + r + 1) * rows_c)
@@ -177,11 +202,19 @@
                     [result[kb * f_block:(kb + 1) * f_block, lanes] for kb in range(pair * bands)], 1)
         start(2, q)
 
-    for q in range(chunks):
+    def first_inverse(q):
         arrived(2, q)
-        result = matmul(ia[...], r3[q].reshape(4 * half, packed))
+        result = from_left(ia, r3[q].reshape(4 * half, packed))
         s4[q] = result.reshape(slabs, 2, rows_a, packed)
         start(3, q)
+
+    for step in range(chunks + 2):
+        if step >= 2:
+            first_inverse(step - 2)
+        if step < chunks:
+            first_forward(step)
+        if 1 <= step <= chunks:
+            second(step - 1)
 
     for q in range(chunks):
         arrived(3, q)
@@ -199,28 +232,33 @@
 
     sums[...] = jnp.zeros_like(sums)
 
-    def inverse_line(a, carry):
-        at = pl.multiple_of(a * modes_x, modes_x)
-        spectrum = jnp.concatenate(
-            [back[t, pl.ds(at, modes_x), 0:min(128, wide - t * 128)] for t in range(back.shape[0])], 1)
-        kinetic_part = matmul(spectrum, ix[...], ((0,), (0,)))
-        level = potential[pl.ds(a, 1)].reshape(rows_c, length)
-        filtered = []
-        for b in range(bands):
-            orbital = orbitals[b, pl.ds(a, 1)].reshape(rows_c, length)
-            applied = kinetic_part[b * rows_c:(b + 1) * rows_c] + level * orbital
-            value = jnp.where(unlocked[b] == 1, (applied - orbital) / 1.5, orbital)
-            out[b, pl.ds(a, 1)] = value.reshape(1, rows_c, length)
-            filtered.append(value)
-        n = 0
-        for b in range(bands):
-            for e in range(b + 1):
-                product = filtered[b] * filtered[e]
-                sums[n] += product.reshape(rows_c // 8, 8, length).sum(0)
-                n += 1
+    def inverse_lines(g, carry):
+        spectra = []
+        for n in range(group):
+            at = pl.multiple_of((g * group + n) * modes_x, modes_x)
+            spectra.append(jnp.concatenate(
+                [back[t, pl.ds(at, modes_x), 0:min(128, wide - t * 128)] for t in range(back.shape[0])], 1).T)
+        kinetic_parts = from_right(jnp.concatenate(spectra, 0), ix)
+        for n in range(group):
+            a = g * group + n
+            kinetic_part = kinetic_parts[n * wide:(n + 1) * wide]
+            level = potential[pl.ds(a, 1)].reshape(rows_c, length)
+            filtered = []
+            for b in range(bands):
+                orbital = orbitals[b, pl.ds(a, 1)].reshape(rows_c, length)
+                applied = kinetic_part[b * rows_c:(b + 1) * rows_c] + level * orbital
+                value = jnp.where(unlocked[b] == 1, (applied - orbital) / 1.5, orbital)
+                out[b, pl.ds(a, 1)] = value.reshape(1, rows_c, length)
+                filtered.append(value)
+            i = 0
+            for b in range(bands):
+                for e in range(b + 1):
+                    squares = filtered[b] * filtered[e]
+                    sums[i] += squares.reshape(rows_c // 8, 8, length).sum(0)
+                    i += 1
         return carry
 
-    lax.fori_loop(0, rows_a, inverse_line, 0)
+    lax.fori_loop(0, rows_a // group, inverse_lines, 0)
 
     total = jnp.sum(jnp.sum(sums[...], axis=1), axis=1, keepdims=True)
     g1[...] = jnp.broadcast_to(total, g1.shape)

time: 105 us -> 93.6 us (0.89)
  Pallas kernels: 100 us -> 88.6 us
    pallas_call x1, Pallas kernels: 100 us -> 88.6 us  [by_kernel(): pl.pallas_call(functools.partial(kernel, (slabs, pencils, chunks, pair, b...]
where the time goes in v2:
time: 93.6 us; the launch traced here: 93.5 us
  Pallas kernels  88.6 us (95%)
  local copies, waits for them, and re-layouts  4.89 us (5%)
    pallas_call x1, Pallas kernels, by_kernel(): pl.pallas_call(functools.partial(kernel, (slabs, pencils, chunks, pair, b...  88.6 us
    unnamed x1, local copies, waits for them, and re-layouts  4.89 us

profile of v2, /device:TPU:0, one launch (start us, length us, event | category | flops | bytes accessed | tf_op | source)
XLA Modules:
  0.0 93.5 jit_solution(8182993066975049244)
XLA Ops:
  0.0 88.6 %shard_map.118 = f32[4,24,48,192]{3,2,1,0:T(8,128)} custom-call(s32[4]{0:T(128)} %unlocked.1, f32[4,24,48,192]{3,2,1,0:T(8,128)} %orbitals.1, f32[24,48,192]{2,1,0:T(8,128)} %potential.1, bf16[2,192,96]{2,1,0:T(8,128)(2,1)} %constant.18.clone.fx, bf16[2,192,384]{2,1,0:T(8,128)(2,1)} %constant.19.clone.fa, bf16[2,384,192]{2,1,0:T(8,128)(2,1)} %constant.20.clone.fc, ...), custom_call_target="tpu_custom_call" | custom-call | flops 1019215872 | bytes 10485760 | tf_op jit(solution)/shard_map/pallas_call | solution.py:350
  88.6 4.9 %copy.14 = f32[4,24,48,192]{3,2,1,0:T(8,128)} copy(f32[4,24,48,192]{3,2,1,0:T(8,128)} %shard_map.118) | data formatting | bytes 7077888

commit v3 on v2

--- a/solution.py
+++ b/solution.py
@@ -36,13 +36,11 @@
     cosine, sine = waves(modes)
     forward = np.stack([np.stack([cosine, sine], 1), np.stack([-sine, cosine], 1)], 0)
     inverse = np.stack([np.stack([cosine.T, -sine.T], 1), np.stack([sine.T, cosine.T], 1)], 0)
-    f_block = 2 * half // pencils
-    a_block = length // slabs
     c_block = length // pencils
-    forward_a = forward.reshape(2, pencils, f_block, 2 * length).transpose(1, 0, 2, 3).reshape(4 * half, 2 * length)
+    forward_a = np.concatenate([cosine, sine], 0)
     forward_c = forward.reshape(4 * half, 2 * length).T
     inverse_c = inverse.reshape(2, pencils, c_block, 4 * half).transpose(1, 0, 2, 3).reshape(2 * length, 4 * half).T
-    inverse_a = inverse.reshape(2, slabs, a_block, 4 * half).transpose(1, 0, 2, 3).reshape(2 * length, 4 * half)
+    inverse_a = np.concatenate([cosine.T, sine.T], 0)
     tables = (forward_x, forward_a, forward_c, inverse_c, inverse_a, inverse_x)
     pairs = []
     for table in tables:
@@ -75,11 +73,13 @@
            lines, s1, r1, s2, r2, s3, r3, s4, r4, back, sums, g1, h1, g2, h2,
            own, send1, recv1, send2, recv2, send3, recv3, send4, recv4, gs1, gr1, gs2, gr2):
     slabs, pencils, chunks, pair, bands, length = sizes
+    few = bands // 2
     rows_a = orbitals.shape[1]
     rows_c = orbitals.shape[2]
     half = length // 4
     f_block = 2 * half // pencils
-    wide = bands * rows_c
+    wide = few * rows_c
+    packed = 2 * pair * wide
     i_s = lax.axis_index("slab")
     i_p = lax.axis_index("pencil")
 
@@ -110,17 +110,17 @@
 
     def copies(which, q):
         if which == 0:
-            remote = [to_slab(d, s1.at[q, slab_peer(d)], r1.at[q, :, mine_a, :], send1.at[q, d], recv1.at[q, d])
+            remote = [to_slab(d, s1.at[q, slab_peer(d)], r1.at[q, mine_a, :], send1.at[q, d], recv1.at[q, d])
                       for d in range(1, slabs)]
-            local = pltpu.make_async_copy(s1.at[q, i_s], r1.at[q, :, mine_a, :], own.at[0, q])
+            local = pltpu.make_async_copy(s1.at[q, i_s], r1.at[q, mine_a, :], own.at[0, q])
         elif which == 1:
             remote = [to_pencil(d, s2.at[q, pencil_peer(d)], r2.at[q, i_p], send2.at[q, d], recv2.at[q, d])
                       for d in range(1, pencils)]
             local = pltpu.make_async_copy(s2.at[q, i_p], r2.at[q, i_p], own.at[1, q])
         elif which == 2:
-            remote = [to_pencil(d, s3.at[q, pencil_peer(d)], r3.at[q, :, mine_f, :], send3.at[q, d], recv3.at[q, d])
+            remote = [to_pencil(d, s3.at[q, pencil_peer(d)], r3.at[q, mine_f, :], send3.at[q, d], recv3.at[q, d])
                       for d in range(1, pencils)]
-            local = pltpu.make_async_copy(s3.at[q, i_p], r3.at[q, :, mine_f, :], own.at[2, q])
+            local = pltpu.make_async_copy(s3.at[q, i_p], r3.at[q, mine_f, :], own.at[2, q])
         else:
             remote = [to_slab(d, s4.at[q, slab_peer(d)], r4.at[q, i_s], send4.at[q, d], recv4.at[q, d])
                       for d in range(1, slabs)]
@@ -140,125 +140,125 @@
         local.wait()
 
     modes_x = 2 * half
-
-    group = 4
-
-    def forward_lines(g, carry):
-        rows = jnp.concatenate(
-            [orbitals[:, pl.ds(g * group + n, 1)].reshape(wide, length) for n in range(group)], 0)
-        result = from_right(rows, fx)
-        for n in range(group):
-            turned = result[n * wide:(n + 1) * wide].T
-            at = pl.multiple_of((g * group + n) * modes_x, modes_x)
-            for t in range(lines.shape[0]):
-                low, high = t * 128, min(t * 128 + 128, wide)
-                lines[t, pl.ds(at, modes_x), 0:high - low] = turned[:, low:high]
-        return carry
-
-    lax.fori_loop(0, rows_a // group, forward_lines, 0)
-    pl.semaphore_wait(barrier, slabs - 1 + pencils - 1)
-
-    def line_rows(ref, i):
-        parts = []
-        for t in range(ref.shape[0]):
-            size = min(128, wide - t * 128)
-            parts.append(ref[t, pl.ds(i, rows_a, stride=modes_x), :][:, :size])
-        return parts
-
-    for q in range(chunks):
-        for j in range(slabs):
-            for r in range(2):
-                parts = []
-                for k in range(pair):
-                    parts += line_rows(lines, ((q * slabs + j) * 2 + r) * pair + k)
-                s1[q, j, r] = jnp.concatenate(parts, 1)
-        start(0, q)
-
-    packed = pair * wide
+    group = 8
+
+    def forward_x(h):
+        def body(g, carry):
+            rows = jnp.concatenate(
+                [orbitals[h * few:(h + 1) * few, pl.ds(g * group + n, 1)].reshape(wide, length)
+                 for n in range(group)], 0)
+            result = from_right(rows, fx)
+            for n in range(group):
+                at = pl.multiple_of((g * group + n) * modes_x, modes_x)
+                lines[h, pl.ds(at, modes_x), 0:wide] = result[n * wide:(n + 1) * wide].T
+            return carry
+
+        lax.fori_loop(0, rows_a // group, body, 0)
+
+    def send_lines(h):
+        for q in range(chunks):
+            for j in range(slabs):
+                s1[h * chunks + q, j] = jnp.concatenate(
+                    [lines[h, pl.ds(((q * slabs + j) * 2 + r) * pair + k, rows_a, stride=modes_x), :][:, :wide]
+                     for r in range(2) for k in range(pair)], 1)
+            start(0, h * chunks + q)
+
+    middle = packed // 2
 
     def first_forward(q):
         arrived(0, q)
-        result = from_left(fa, r1[q].reshape(2 * length, packed))
-        s2[q] = result.reshape(pencils, 2, f_block, packed)
+        result = from_left(fa, r1[q])
+        cosine, sine = result[:2 * half], result[2 * half:]
+        result = cosine + jnp.concatenate([sine[:, middle:], -sine[:, :middle]], 1)
+        s2[q] = result.reshape(s2.shape[1:])
         start(1, q)
 
     def second(q):
         arrived(1, q)
         blocks = []
-        for kb in range(pair * bands):
-            lanes = slice(kb * rows_c, (kb + 1) * rows_c)
-            blocks.append(jnp.concatenate([r2[q, p, r, :, lanes] for r in range(2) for p in range(pencils)], 1))
+        for kb in range(pair * few):
+            blocks.append(jnp.concatenate(
+                [r2[q, p, :, r * middle + kb * rows_c:r * middle + (kb + 1) * rows_c]
+                 for r in range(2) for p in range(pencils)], 1))
         spectrum = from_right(jnp.concatenate(blocks, 0), fc)
-        mode_k = row_k[...] + (q * slabs * pair + i_s * pair).astype(jnp.float32)
+        mode_k = row_k[...] + (q % chunks * slabs * pair + i_s * pair).astype(jnp.float32)
         mode_f = row_f[...] + (i_p * f_block - half).astype(jnp.float32)
         squared = mode_k * mode_k + mode_f * mode_f + col_s[...]
         radius = float(half * half)
         kinetic = jnp.where(squared < radius, 4.0 * squared / radius, 0.0) * (1.0 / float(length**3))
         result = from_right(spectrum * kinetic, ic)
         for p in range(pencils):
-            for r in range(2):
-                lanes = slice((p * 2 + r) * rows_c, (p * 2 + r + 1) * rows_c)
-                s3[q, p, r] = jnp.concatenate(
-                    [result[kb * f_block:(kb + 1) * f_block, lanes] for kb in range(pair * bands)], 1)
+            s3[q, p] = jnp.concatenate(
+                [result[kb * f_block:(kb + 1) * f_block, (p * 2 + r) * rows_c:(p * 2 + r + 1) * rows_c]
+                 for r in range(2) for kb in range(pair * few)], 1)
         start(2, q)
 
     def first_inverse(q):
         arrived(2, q)
-        result = from_left(ia, r3[q].reshape(4 * half, packed))
-        s4[q] = result.reshape(slabs, 2, rows_a, packed)
+        result = from_left(ia, r3[q])
+        cosine, sine = result[:length], result[length:]
+        result = cosine + jnp.concatenate([-sine[:, middle:], sine[:, :middle]], 1)
+        s4[q] = result.reshape(s4.shape[1:])
         start(3, q)
 
-    for step in range(chunks + 2):
+    def take_lines(h, q):
+        arrived(3, h * chunks + q)
+        unused = jnp.zeros((rows_a, 128 - wide), jnp.float32)
+        for j in range(slabs):
+            value = r4[h * chunks + q, j]
+            for r in range(2):
+                for k in range(pair):
+                    piece = value[:, r * middle + k * wide:r * middle + (k + 1) * wide]
+                    back[h, pl.ds(((q * slabs + j) * 2 + r) * pair + k, rows_a, stride=modes_x), :] = (
+                        jnp.concatenate([piece, unused], 1))
+
+    def inverse_x(h):
+        def body(g, carry):
+            spectra = []
+            for n in range(group):
+                at = pl.multiple_of((g * group + n) * modes_x, modes_x)
+                spectra.append(back[h, pl.ds(at, modes_x), 0:wide].T)
+            kinetic_parts = from_right(jnp.concatenate(spectra, 0), ix)
+            for n in range(group):
+                a = g * group + n
+                level = potential[pl.ds(a, 1)].reshape(rows_c, length)
+                filtered = [out[b, pl.ds(a, 1)].reshape(rows_c, length) for b in range(h * few)]
+                for b in range(few):
+                    orbital = orbitals[h * few + b, pl.ds(a, 1)].reshape(rows_c, length)
+                    kinetic_part = kinetic_parts[n * wide + b * rows_c:n * wide + (b + 1) * rows_c]
+                    applied = kinetic_part + level * orbital
+                    value = jnp.where(unlocked[h * few + b] == 1, (applied - orbital) / 1.5, orbital)
+                    out[h * few + b, pl.ds(a, 1)] = value.reshape(1, rows_c, length)
+                    filtered.append(value)
+                for b in range(h * few, (h + 1) * few):
+                    for e in range(b + 1):
+                        squares = filtered[b] * filtered[e]
+                        sums[b * (b + 1) // 2 + e] += squares.reshape(rows_c // 8, 8, length).sum(0)
+            return carry
+
+        lax.fori_loop(0, rows_a // group, body, 0)
+
+    sums[...] = jnp.zeros_like(sums)
+    forward_x(0)
+    pl.semaphore_wait(barrier, slabs - 1 + pencils - 1)
+    send_lines(0)
+    forward_x(1)
+    send_lines(1)
+    last = 2 * chunks
+    for step in range(last + 1):
         if step >= 2:
             first_inverse(step - 2)
-        if step < chunks:
+        if step < last:
             first_forward(step)
-        if 1 <= step <= chunks:
+        if step >= 1:
             second(step - 1)
-
     for q in range(chunks):
-        arrived(3, q)
-        for j in range(slabs):
-            for r in range(2):
-                value = r4[q, j, r]
-                for k in range(pair):
-                    i = ((q * slabs + j) * 2 + r) * pair + k
-                    for t in range(back.shape[0]):
-                        low, high = t * 128, min(t * 128 + 128, wide)
-                        piece = value[:, k * wide + low:k * wide + high]
-                        if high - low < 128:
-                            piece = jnp.concatenate([piece, jnp.zeros((rows_a, 128 - high + low), jnp.float32)], 1)
-                        back[t, pl.ds(i, rows_a, stride=modes_x), :] = piece
-
-    sums[...] = jnp.zeros_like(sums)
-
-    def inverse_lines(g, carry):
-        spectra = []
-        for n in range(group):
-            at = pl.multiple_of((g * group + n) * modes_x, modes_x)
-            spectra.append(jnp.concatenate(
-                [back[t, pl.ds(at, modes_x), 0:min(128, wide - t * 128)] for t in range(back.shape[0])], 1).T)
-        kinetic_parts = from_right(jnp.concatenate(spectra, 0), ix)
-        for n in range(group):
-            a = g * group + n
-            kinetic_part = kinetic_parts[n * wide:(n + 1) * wide]
-            level = potential[pl.ds(a, 1)].reshape(rows_c, length)
-            filtered = []
-            for b in range(bands):
-                orbital = orbitals[b, pl.ds(a, 1)].reshape(rows_c, length)
-                applied = kinetic_part[b * rows_c:(b + 1) * rows_c] + level * orbital
-                value = jnp.where(unlocked[b] == 1, (applied - orbital) / 1.5, orbital)
-                out[b, pl.ds(a, 1)] = value.reshape(1, rows_c, length)
-                filtered.append(value)
-            i = 0
-            for b in range(bands):
-                for e in range(b + 1):
-                    squares = filtered[b] * filtered[e]
-                    sums[i] += squares.reshape(rows_c // 8, 8, length).sum(0)
-                    i += 1
-        return carry
-
-    lax.fori_loop(0, rows_a // group, inverse_lines, 0)
+        take_lines(0, q)
+    first_inverse(last - 1)
+    inverse_x(0)
+    for q in range(chunks):
+        take_lines(1, q)
+    inverse_x(1)
 
     total = jnp.sum(jnp.sum(sums[...], axis=1), axis=1, keepdims=True)
     g1[...] = jnp.broadcast_to(total, g1.shape)
@@ -300,7 +300,7 @@
 
     lax.fori_loop(0, rows_a, solve_line, 0)
     for which in range(4):
-        for q in range(chunks):
+        for q in range(2 * chunks):
             for copy in copies(which, q)[0]:
                 copy.wait_send()
 
@@ -310,43 +310,43 @@
     half = length // 4
     pair = half // (slabs * chunks)
     f_block = 2 * half // pencils
-    wide = bands * rows_c
-    packed = pair * wide
-    tiles = -(-wide // 128)
+    few = bands // 2
+    parts = 2 * chunks
+    packed = 2 * pair * few * rows_c
     pairs = bands * (bands + 1) // 2
     tables = dft_tables(length, slabs, pencils, chunks)
-    rows = np.arange(pair * bands * f_block)
-    row_k = (rows // (bands * f_block)).astype(np.float32)[:, None]
+    rows = np.arange(pair * few * f_block)
+    row_k = (rows // (few * f_block)).astype(np.float32)[:, None]
     row_f = (rows % f_block).astype(np.float32)[:, None]
     col_s = ((np.arange(4 * half) % (2 * half) - half).astype(np.float32) ** 2)[None, :]
     vmem = pl.BlockSpec(memory_space=pltpu.VMEM)
     f32 = jnp.float32
     dma = pltpu.SemaphoreType.DMA
     scratch = [
-        pltpu.VMEM((tiles, rows_a * 2 * half, 128), f32),
-        pltpu.VMEM((chunks, slabs, 2, rows_a, packed), f32),
-        pltpu.VMEM((chunks, 2, length, packed), f32),
-        pltpu.VMEM((chunks, pencils, 2, f_block, packed), f32),
-        pltpu.VMEM((chunks, pencils, 2, f_block, packed), f32),
-        pltpu.VMEM((chunks, pencils, 2, f_block, packed), f32),
-        pltpu.VMEM((chunks, 2, 2 * half, packed), f32),
-        pltpu.VMEM((chunks, slabs, 2, rows_a, packed), f32),
-        pltpu.VMEM((chunks, slabs, 2, rows_a, packed), f32),
-        pltpu.VMEM((tiles, rows_a * 2 * half, 128), f32),
+        pltpu.VMEM((2, rows_a * 2 * half, 128), f32),
+        pltpu.VMEM((parts, slabs, rows_a, packed), f32),
+        pltpu.VMEM((parts, length, packed), f32),
+        pltpu.VMEM((parts, pencils, f_block, packed), f32),
+        pltpu.VMEM((parts, pencils, f_block, packed), f32),
+        pltpu.VMEM((parts, pencils, f_block, packed), f32),
+        pltpu.VMEM((parts, 2 * half, packed), f32),
+        pltpu.VMEM((parts, slabs, rows_a, packed), f32),
+        pltpu.VMEM((parts, slabs, rows_a, packed), f32),
+        pltpu.VMEM((2, rows_a * 2 * half, 128), f32),
         pltpu.VMEM((pairs, 8, length), f32),
         pltpu.VMEM((pairs, 128), f32),
         pltpu.VMEM((slabs, pairs, 128), f32),
         pltpu.VMEM((pairs, 128), f32),
         pltpu.VMEM((pencils, pairs, 128), f32),
-        dma((4, chunks)),
-        dma((chunks, slabs)), dma((chunks, slabs)),
-        dma((chunks, pencils)), dma((chunks, pencils)),
-        dma((chunks, pencils)), dma((chunks, pencils)),
-        dma((chunks, slabs)), dma((chunks, slabs)),
+        dma((4, parts)),
+        dma((parts, slabs)), dma((parts, slabs)),
+        dma((parts, pencils)), dma((parts, pencils)),
+        dma((parts, pencils)), dma((parts, pencils)),
+        dma((parts, slabs)), dma((parts, slabs)),
         dma((slabs,)), dma((slabs,)),
         dma((pencils,)), dma((pencils,)),
     ]
-    flops = 2 * rows_a * wide * length * 2 * half * 6
+    flops = 2 * rows_a * bands * rows_c * length * 2 * half * 6
     return pl.pallas_call(
         functools.partial(kernel, (slabs, pencils, chunks, pair, bands, length)),
         out_shape=jax.ShapeDtypeStruct(orbitals.shape, f32),
@@ -465,7 +465,8 @@
         half = length // 4
         f_block = 2 * half // pencils
         chunks = half // (2 * slabs)
-        fits = chunks > 0 and half % (2 * slabs) == 0 and rows_a % 8 == 0 and rows_c % 8 == 0 and f_block % 8 == 0
+        even = bands % 2 == 0 and bands // 2 * rows_c <= 128 and chunks > 0 and half % (2 * slabs) == 0
+        fits = even and rows_a % 8 == 0 and rows_c % 8 == 0 and f_block % 8 == 0
         if fits:
             return by_kernel(slabs, pencils, chunks, orbitals, potential, unlocked)
         return by_collectives(orbitals, potential, unlocked)

time: 93.6 us -> 93.1 us (level)
  no operation moved by 1% of the time
where the time goes in v3:
time: 93.1 us; the launch traced here: 93 us
  Pallas kernels  88.1 us (95%)
  local copies, waits for them, and re-layouts  4.89 us (5%)
    pallas_call x1, Pallas kernels, by_kernel(): pl.pallas_call(functools.partial(kernel, (slabs, pencils, chunks, pair, b...  88.1 us
    unnamed x1, local copies, waits for them, and re-layouts  4.89 us

profile of v3, /device:TPU:0, one launch (start us, length us, event | category | flops | bytes accessed | tf_op | source)
XLA Modules:
  0.0 93.0 jit_solution(3545375020088255658)
XLA Ops:
  0.0 88.1 %shard_map.118 = f32[4,24,48,192]{3,2,1,0:T(8,128)} custom-call(s32[4]{0:T(128)} %unlocked.1, f32[4,24,48,192]{3,2,1,0:T(8,128)} %orbitals.1, f32[24,48,192]{2,1,0:T(8,128)} %potential.1, bf16[2,192,96]{2,1,0:T(8,128)(2,1)} %constant.18.clone.fx, bf16[2,192,192]{2,1,0:T(8,128)(2,1)} %constant.19.clone.fa, bf16[2,384,192]{2,1,0:T(8,128)(2,1)} %constant.20.clone.fc, ...), custom_call_target="tpu_custom_call" | custom-call | flops 1019215872 | bytes 10485760 | tf_op jit(solution)/shard_map/pallas_call | solution.py:350
  88.1 4.9 %copy.14 = f32[4,24,48,192]{3,2,1,0:T(8,128)} copy(f32[4,24,48,192]{3,2,1,0:T(8,128)} %shard_map.118) | data formatting | bytes 7077888

commit v4 on v3

--- a/solution.py
+++ b/solution.py
@@ -161,12 +161,15 @@
                 s1[h * chunks + q, j] = jnp.concatenate(
                     [lines[h, pl.ds(((q * slabs + j) * 2 + r) * pair + k, rows_a, stride=modes_x), :][:, :wide]
                      for r in range(2) for k in range(pair)], 1)
-            start(0, h * chunks + q)
+            if h == 0:
+                start(0, q)
 
     middle = packed // 2
 
     def first_forward(q):
         arrived(0, q)
+        if q + chunks < 2 * chunks:
+            start(0, q + chunks)
         result = from_left(fa, r1[q])
         cosine, sine = result[:2 * half], result[2 * half:]
         result = cosine + jnp.concatenate([sine[:, middle:], -sine[:, :middle]], 1)
@@ -246,12 +249,12 @@
     send_lines(1)
     last = 2 * chunks
     for step in range(last + 1):
-        if step >= 2:
-            first_inverse(step - 2)
         if step < last:
             first_forward(step)
         if step >= 1:
             second(step - 1)
+        if step >= 2:
+            first_inverse(step - 2)
     for q in range(chunks):
         take_lines(0, q)
     first_inverse(last - 1)

time: 93.1 us -> 82.4 us (0.89)
  Pallas kernels: 88.1 us -> 77.4 us
    pallas_call x1, Pallas kernels: 88.1 us -> 77.4 us  [by_kernel(): pl.pallas_call(functools.partial(kernel, (slabs, pencils, chunks, pair, b...]
where the time goes in v4:
time: 82.4 us; the launch traced here: 82.3 us
  Pallas kernels  77.4 us (94%)
  local copies, waits for them, and re-layouts  4.89 us (6%)
    pallas_call x1, Pallas kernels, by_kernel(): pl.pallas_call(functools.partial(kernel, (slabs, pencils, chunks, pair, b...  77.4 us
    unnamed x1, local copies, waits for them, and re-layouts  4.89 us

profile of v4, /device:TPU:0, one launch (start us, length us, event | category | flops | bytes accessed | tf_op | source)
XLA Modules:
  0.0 82.3 jit_solution(3679918178661350136)
XLA Ops:
  0.0 77.4 %shard_map.118 = f32[4,24,48,192]{3,2,1,0:T(8,128)} custom-call(s32[4]{0:T(128)} %unlocked.1, f32[4,24,48,192]{3,2,1,0:T(8,128)} %orbitals.1, f32[24,48,192]{2,1,0:T(8,128)} %potential.1, bf16[2,192,96]{2,1,0:T(8,128)(2,1)} %constant.18.clone.fx, bf16[2,192,192]{2,1,0:T(8,128)(2,1)} %constant.19.clone.fa, bf16[2,384,192]{2,1,0:T(8,128)(2,1)} %constant.20.clone.fc, ...), custom_call_target="tpu_custom_call" | custom-call | flops 1019215872 | bytes 10485760 | tf_op jit(solution)/shard_map/pallas_call | solution.py:353
  77.4 4.9 %copy.14 = f32[4,24,48,192]{3,2,1,0:T(8,128)} copy(f32[4,24,48,192]{3,2,1,0:T(8,128)} %shard_map.118) | data formatting | bytes 7077888

commit v5 on v4

--- a/solution.py
+++ b/solution.py
@@ -69,8 +69,8 @@
     return product(high, table[0]) + (product(low, table[0]) + product(high, table[1]))
 
 
-def kernel(sizes, unlocked, orbitals, potential, fx, fa, fc, ic, ia, ix, row_k, row_f, col_s, out,
-           lines, s1, r1, s2, r2, s3, r3, s4, r4, back, sums, g1, h1, g2, h2,
+def kernel(sizes, unlocked, given, given_potential, fx, fa, fc, ic, ia, ix, row_k, row_f, col_s, kept, solver,
+           orbitals, potential, out, load, store, lines, s1, r1, s2, r2, s3, r3, s4, r4, back, sums, g1, h1, g2, h2,
            own, send1, recv1, send2, recv2, send3, recv3, send4, recv4, gs1, gr1, gs2, gr2):
     slabs, pencils, chunks, pair, bands, length = sizes
     few = bands // 2
@@ -88,6 +88,21 @@
 
     def pencil_peer(d):
         return lax.rem(i_p + d, pencils)
+
+    group = 8
+
+    def fetch(h, g):
+        at = (pl.ds(h * few, few), pl.ds(pl.multiple_of(g * group, group), group))
+        return pltpu.make_async_copy(given.at[at], orbitals.at[at], load.at[h, g])
+
+    fetch_potential = pltpu.make_async_copy(given_potential, potential, load.at[2, 0])
+    for h in range(2):
+        for g in range(rows_a // group):
+            fetch(h, g).start()
+    fetch_potential.start()
+
+    def keep(h):
+        return pltpu.make_async_copy(out.at[pl.ds(h * few, few)], kept.at[pl.ds(h * few, few)], store.at[h])
 
     barrier = pltpu.get_barrier_semaphore()
     for d in range(1, slabs):
@@ -140,10 +155,10 @@
         local.wait()
 
     modes_x = 2 * half
-    group = 8
 
     def forward_x(h):
         def body(g, carry):
+            fetch(h, g).wait()
             rows = jnp.concatenate(
                 [orbitals[h * few:(h + 1) * few, pl.ds(g * group + n, 1)].reshape(wide, length)
                  for n in range(group)], 0)
@@ -258,10 +273,13 @@
     for q in range(chunks):
         take_lines(0, q)
     first_inverse(last - 1)
+    fetch_potential.wait()
     inverse_x(0)
+    keep(0).start()
     for q in range(chunks):
         take_lines(1, q)
     inverse_x(1)
+    keep(1).start()
 
     total = jnp.sum(jnp.sum(sums[...], axis=1), axis=1, keepdims=True)
     g1[...] = jnp.broadcast_to(total, g1.shape)
@@ -288,24 +306,29 @@
             for m in range(e):
                 value = value - factor[b, m] * factor[e, m]
             factor[b, e] = jnp.sqrt(value) if b == e else value / factor[e, e]
-    inverse = [1.0 / factor[b, b] for b in range(bands)]
-
-    def solve_line(a, carry):
-        solved = []
-        for b in range(bands):
-            value = out[b, pl.ds(a, 1)].reshape(rows_c, length)
-            for m in range(b):
-                value = value - factor[b, m] * solved[m]
-            value = value * inverse[b]
-            out[b, pl.ds(a, 1)] = value.reshape(1, rows_c, length)
-            solved.append(value)
-        return carry
-
-    lax.fori_loop(0, rows_a, solve_line, 0)
+    entries = [1.0 / factor[b, e] if b == e else factor[b, e] for b in range(bands) for e in range(b + 1)]
+    for n, entry in enumerate(entries):
+        solver[n:n + 1, :] = jnp.broadcast_to(entry, (1, 128))
+    for h in range(2):
+        keep(h).wait()
     for which in range(4):
         for q in range(2 * chunks):
             for copy in copies(which, q)[0]:
                 copy.wait_send()
+
+
+def solve(solver, filtered, out):
+    bands, rows_a, rows_c, length = filtered.shape
+    for a in range(rows_a):
+        solved = []
+        for b in range(bands):
+            value = filtered[b, a]
+            first = b * (b + 1) // 2
+            for m in range(b):
+                value = value - solver[first + m:first + m + 1, 0:1] * solved[m]
+            value = value * solver[first + b:first + b + 1, 0:1]
+            out[b, a] = value
+            solved.append(value)
 
 
 def by_kernel(slabs, pencils, chunks, orbitals, potential, unlocked):
@@ -326,6 +349,11 @@
     f32 = jnp.float32
     dma = pltpu.SemaphoreType.DMA
     scratch = [
+        pltpu.VMEM(orbitals.shape, f32),
+        pltpu.VMEM(potential.shape, f32),
+        pltpu.VMEM(orbitals.shape, f32),
+        dma((3, rows_a // 8)),
+        dma((2,)),
         pltpu.VMEM((2, rows_a * 2 * half, 128), f32),
         pltpu.VMEM((parts, slabs, rows_a, packed), f32),
         pltpu.VMEM((parts, length, packed), f32),
@@ -350,17 +378,28 @@
         dma((pencils,)), dma((pencils,)),
     ]
     flops = 2 * rows_a * bands * rows_c * length * 2 * half * 6
-    return pl.pallas_call(
+    anywhere = pl.BlockSpec(memory_space=pl.ANY)
+    filtered, solver = pl.pallas_call(
         functools.partial(kernel, (slabs, pencils, chunks, pair, bands, length)),
-        out_shape=jax.ShapeDtypeStruct(orbitals.shape, f32),
-        in_specs=[pl.BlockSpec(memory_space=pltpu.SMEM)] + [vmem] * 11,
-        out_specs=vmem,
+        out_shape=[jax.ShapeDtypeStruct(orbitals.shape, f32), jax.ShapeDtypeStruct((pairs, 128), f32)],
+        in_specs=[pl.BlockSpec(memory_space=pltpu.SMEM), anywhere, anywhere] + [vmem] * 9,
+        out_specs=[anywhere, vmem],
         scratch_shapes=scratch,
         compiler_params=pltpu.CompilerParams(
             collective_id=0, has_side_effects=True, vmem_limit_bytes=56 * 1024 * 1024),
         cost_estimate=pl.CostEstimate(flops=flops, bytes_accessed=10 * 2**20, transcendentals=0),
     )(unlocked, orbitals, potential, *[jnp.asarray(t) for t in tables],
       jnp.asarray(row_k), jnp.asarray(row_f), jnp.asarray(col_s))
+    planes = 4
+    block = pl.BlockSpec((bands, planes, rows_c, length), lambda i: (0, i, 0, 0))
+    return pl.pallas_call(
+        solve,
+        grid=(rows_a // planes,),
+        out_shape=jax.ShapeDtypeStruct(orbitals.shape, f32),
+        in_specs=[pl.BlockSpec((pairs, 128), lambda i: (0, 0)), block],
+        out_specs=block,
+        cost_estimate=pl.CostEstimate(flops=20 * orbitals.size, bytes_accessed=8 * orbitals.size, transcendentals=0),
+    )(solver, filtered)
 
 
 NG = 192

time: 82.4 us -> 80.1 us (0.972)
  local copies, waits for them, and re-layouts: 4.89 us -> 0 us
  Pallas kernels: 77.4 us -> 79.9 us
    pallas_call x0 -> x1, Pallas kernels: none -> 6.31 us  [by_kernel(): pl.pallas_call(solve, grid=(rows_a // planes,), out_shape=jax.ShapeDtypeS...]
    unnamed x1 -> x0, local copies, waits for them, and re-layouts: 4.89 us -> none
    pallas_call x1, Pallas kernels: 77.4 us -> 73.6 us  [by_kernel(): pl.pallas_call(functools.partial(kernel, (slabs, pencils, chunks, pair, b...]
where the time goes in v5:
time: 80.1 us; the launch traced here: 79.9 us
  Pallas kernels  79.9 us (100%)
    pallas_call x1, Pallas kernels, by_kernel(): pl.pallas_call(functools.partial(kernel, (slabs, pencils, chunks, pair, b...  73.6 us
    pallas_call x1, Pallas kernels, by_kernel(): pl.pallas_call(solve, grid=(rows_a // planes,), out_shape=jax.ShapeDtypeS...  6.31 us

profile of v5, /device:TPU:0, one launch (start us, length us, event | category | flops | bytes accessed | tf_op | source)
XLA Modules:
  0.0 79.9 jit_solution(7719300635854085076)
XLA Ops:
  0.0 73.6 %shard_map.118 = (f32[4,24,48,192]{3,2,1,0:T(8,128)}, f32[10,128]{1,0:T(8,128)}) custom-call(s32[4]{0:T(128)} %unlocked.1, f32[4,24,48,192]{3,2,1,0:T(8,128)} %given.1, f32[24,48,192]{2,1,0:T(8,128)} %given_potential.1, bf16[2,192,96]{2,1,0:T(8,128)(2,1)} %constant.18.clone.fx, bf16[2,192,192]{2,1,0:T(8,128)(2,1)} %constant.19.clone.fa, ...), custom_call_target="tpu_custom_call" | custom-call | flops 1019215872 | bytes 10485760 | tf_op jit(solution)/shard_map/pallas_call | solution.py:382
  73.6 6.3 %shard_map.119 = f32[4,24,48,192]{3,2,1,0:T(8,128)} custom-call(f32[10,128]{1,0:T(8,128)} %get-tuple-element.7.solver, f32[4,24,48,192]{3,2,1,0:T(8,128)} %get-tuple-element.8.filtered), custom_call_target="tpu_custom_call" | custom-call | flops 17694720 | bytes 7077888 | tf_op jit(solution)/shard_map/pallas_call | solution.py:395

commit v6 on v5

--- a/solution.py
+++ b/solution.py
@@ -170,26 +170,24 @@
 
         lax.fori_loop(0, rows_a // group, body, 0)
 
-    def send_lines(h):
-        for q in range(chunks):
-            for j in range(slabs):
-                s1[h * chunks + q, j] = jnp.concatenate(
-                    [lines[h, pl.ds(((q * slabs + j) * 2 + r) * pair + k, rows_a, stride=modes_x), :][:, :wide]
-                     for r in range(2) for k in range(pair)], 1)
-            if h == 0:
-                start(0, q)
+    def send_lines(h, q):
+        for j in range(slabs):
+            s1[h * chunks + q, j] = jnp.concatenate(
+                [lines[h, pl.ds(((q * slabs + j) * 2 + r) * pair + k, rows_a, stride=modes_x), :][:, :wide]
+                 for r in range(2) for k in range(pair)], 1)
+        start(0, h * chunks + q)
 
     middle = packed // 2
 
     def first_forward(q):
         arrived(0, q)
-        if q + chunks < 2 * chunks:
-            start(0, q + chunks)
         result = from_left(fa, r1[q])
         cosine, sine = result[:2 * half], result[2 * half:]
         result = cosine + jnp.concatenate([sine[:, middle:], -sine[:, :middle]], 1)
         s2[q] = result.reshape(s2.shape[1:])
         start(1, q)
+        if q < chunks:
+            send_lines(1, q)
 
     def second(q):
         arrived(1, q)
@@ -230,7 +228,7 @@
                     back[h, pl.ds(((q * slabs + j) * 2 + r) * pair + k, rows_a, stride=modes_x), :] = (
                         jnp.concatenate([piece, unused], 1))
 
-    def inverse_x(h):
+    def inverse_x(h, first, end):
         def body(g, carry):
             spectra = []
             for n in range(group):
@@ -254,14 +252,14 @@
                         sums[b * (b + 1) // 2 + e] += squares.reshape(rows_c // 8, 8, length).sum(0)
             return carry
 
-        lax.fori_loop(0, rows_a // group, body, 0)
+        lax.fori_loop(first, end, body, 0)
 
     sums[...] = jnp.zeros_like(sums)
     forward_x(0)
     pl.semaphore_wait(barrier, slabs - 1 + pencils - 1)
-    send_lines(0)
+    for q in range(chunks):
+        send_lines(0, q)
     forward_x(1)
-    send_lines(1)
     last = 2 * chunks
     for step in range(last + 1):
         if step < last:
@@ -270,15 +268,19 @@
             second(step - 1)
         if step >= 2:
             first_inverse(step - 2)
-    for q in range(chunks):
-        take_lines(0, q)
+        if step >= last - 1:
+            for q in range(chunks - 1) if step < last else range(chunks - 1, chunks):
+                take_lines(0, q)
+    groups = rows_a // group
+    early = groups - groups // 3
+    fetch_potential.wait()
+    inverse_x(0, 0, early)
     first_inverse(last - 1)
-    fetch_potential.wait()
-    inverse_x(0)
+    inverse_x(0, early, groups)
     keep(0).start()
     for q in range(chunks):
         take_lines(1, q)
-    inverse_x(1)
+    inverse_x(1, 0, groups)
     keep(1).start()
 
     total = jnp.sum(jnp.sum(sums[...], axis=1), axis=1, keepdims=True)
@@ -325,8 +327,8 @@
             value = filtered[b, a]
             first = b * (b + 1) // 2
             for m in range(b):
-                value = value - solver[first + m:first + m + 1, 0:1] * solved[m]
-            value = value * solver[first + b:first + b + 1, 0:1]
+                value = value - solver[first + m, 0] * solved[m]
+            value = value * solver[first + b, 0]
             out[b, a] = value
             solved.append(value)
 
@@ -396,7 +398,7 @@
         solve,
         grid=(rows_a // planes,),
         out_shape=jax.ShapeDtypeStruct(orbitals.shape, f32),
-        in_specs=[pl.BlockSpec((pairs, 128), lambda i: (0, 0)), block],
+        in_specs=[pl.BlockSpec(memory_space=pltpu.SMEM), block],
         out_specs=block,
         cost_estimate=pl.CostEstimate(flops=20 * orbitals.size, bytes_accessed=8 * orbitals.size, transcendentals=0),
     )(solver, filtered)

time: 80.1 us -> 80.1 us (level)
  no operation moved by 1% of the time
where the time goes in v6:
time: 80.1 us; the launch traced here: 79.8 us
  Pallas kernels  79.8 us (100%)
    pallas_call x1, Pallas kernels, by_kernel(): pl.pallas_call(functools.partial(kernel, (slabs, pencils, chunks, pair, b...  73.6 us
    pallas_call x1, Pallas kernels, by_kernel(): pl.pallas_call(solve, grid=(rows_a // planes,), out_shape=jax.ShapeDtypeS...  6.22 us

profile of v6, /device:TPU:0, one launch (start us, length us, event | category | flops | bytes accessed | tf_op | source)
XLA Modules:
  0.0 79.8 jit_solution(16720175196972952160)
XLA Ops:
  0.0 73.6 %shard_map.118 = (f32[4,24,48,192]{3,2,1,0:T(8,128)}, f32[10,128]{1,0:T(8,128)}) custom-call(s32[4]{0:T(128)} %unlocked.1, f32[4,24,48,192]{3,2,1,0:T(8,128)} %given.1, f32[24,48,192]{2,1,0:T(8,128)} %given_potential.1, bf16[2,192,96]{2,1,0:T(8,128)(2,1)} %constant.18.clone.fx, bf16[2,192,192]{2,1,0:T(8,128)(2,1)} %constant.19.clone.fa, ...), custom_call_target="tpu_custom_call" | custom-call | flops 1019215872 | bytes 10485760 | tf_op jit(solution)/shard_map/pallas_call | solution.py:384
  73.6 6.2 %shard_map.119 = f32[4,24,48,192]{3,2,1,0:T(8,128)} custom-call(f32[10,128]{1,0:T(8,128)} %get-tuple-element.7.solver, f32[4,24,48,192]{3,2,1,0:T(8,128)} %get-tuple-element.8.filtered), custom_call_target="tpu_custom_call" | custom-call | flops 17694720 | bytes 7077888 | tf_op jit(solution)/shard_map/pallas_call | solution.py:397

commit v7 on v6

--- a/solution.py
+++ b/solution.py
@@ -384,15 +384,15 @@
     filtered, solver = pl.pallas_call(
         functools.partial(kernel, (slabs, pencils, chunks, pair, bands, length)),
         out_shape=[jax.ShapeDtypeStruct(orbitals.shape, f32), jax.ShapeDtypeStruct((pairs, 128), f32)],
-        in_specs=[pl.BlockSpec(memory_space=pltpu.SMEM), anywhere, anywhere] + [vmem] * 9,
+        in_specs=[pl.BlockSpec(memory_space=pltpu.SMEM)] + [pl.BlockSpec(memory_space=pltpu.HBM)] * 2 + [vmem] * 9,
         out_specs=[anywhere, vmem],
         scratch_shapes=scratch,
         compiler_params=pltpu.CompilerParams(
-            collective_id=0, has_side_effects=True, vmem_limit_bytes=56 * 1024 * 1024),
+            collective_id=0, has_side_effects=True, vmem_limit_bytes=36 * 1024 * 1024),
         cost_estimate=pl.CostEstimate(flops=flops, bytes_accessed=10 * 2**20, transcendentals=0),
     )(unlocked, orbitals, potential, *[jnp.asarray(t) for t in tables],
       jnp.asarray(row_k), jnp.asarray(row_f), jnp.asarray(col_s))
-    planes = 4
+    planes = 8
     block = pl.BlockSpec((bands, planes, rows_c, length), lambda i: (0, i, 0, 0))
     return pl.pallas_call(
         solve,

time: 80.1 us -> 93.3 us (1.16)
  local copies, waits for them, and re-layouts: 0 us -> 14.8 us
  Pallas kernels: 79.8 us -> 77.9 us
    unnamed x0 -> x28, local copies, waits for them, and re-layouts: none -> 14.8 us
    pallas_call x1, Pallas kernels: 73.6 us -> 72.2 us  [by_kernel(): pl.pallas_call(functools.partial(kernel, (slabs, pencils, chunks, pair, b...]
where the time goes in v7:
time: 93.3 us; the launch traced here: 92.8 us
  Pallas kernels  77.9 us (83%)
  local copies, waits for them, and re-layouts  14.8 us (16%)
    pallas_call x1, Pallas kernels, by_kernel(): pl.pallas_call(functools.partial(kernel, (slabs, pencils, chunks, pair, b...  72.2 us
    unnamed x28, local copies, waits for them, and re-layouts  14.8 us
    pallas_call x1, Pallas kernels, by_kernel(): pl.pallas_call(solve, grid=(rows_a // planes,), out_shape=jax.ShapeDtypeS...  5.64 us

profile of v7, /device:TPU:0, one launch (start us, length us, event | category | flops | bytes accessed | tf_op | source)
XLA Modules:
  0.0 92.8 jit_solution(16251165645294894045)
XLA Ops:
  0.0 0.0 copy-start
  0.0 2.3 %copy-done = f32[4,24,48,192]{3,2,1,0:T(8,128)S(1)} copy-done((f32[4,24,48,192]{3,2,1,0:T(8,128)S(1)}, f32[4,24,48,192]{3,2,1,0:T(8,128)}, u32[]{:S(2)}) %copy-start) | copy-done | bytes 3538968
  2.3 0.0 copy-start.2
  2.3 1.3 %copy-done.2 = f32[24,48,192]{2,1,0:T(8,128)S(1)} copy-done((f32[24,48,192]{2,1,0:T(8,128)S(1)}, f32[24,48,192]{2,1,0:T(8,128)}, u32[]{:S(2)}) %copy-start.2) | copy-done | bytes 884760
  3.6 0.0 copy-start.3
  3.6 1.0 %copy-done.3 = bf16[2,384,192]{2,1,0:T(8,128)(2,1)S(1)} copy-done((bf16[2,384,192]{2,1,0:T(8,128)(2,1)S(1)}, bf16[2,384,192]{2,1,0:T(8,128)(2,1)}, u32[]{:S(2)}) %copy-start.3) | copy-done | bytes 294936
  4.6 0.0 copy-start.4
  4.6 1.0 %copy-done.4 = bf16[2,192,384]{2,1,0:T(8,128)(2,1)S(1)} copy-done((bf16[2,192,384]{2,1,0:T(8,128)(2,1)S(1)}, bf16[2,192,384]{2,1,0:T(8,128)(2,1)}, u32[]{:S(2)}) %copy-start.4) | copy-done | bytes 294936
  5.6 0.0 copy-start.5
  5.6 0.9 copy-done.5
  6.5 0.0 copy-start.6
  6.5 0.9 copy-done.6
  7.4 0.0 copy-start.7
  7.4 0.9 copy-done.7
  8.3 0.0 copy-start.8
  8.3 0.9 copy-done.8
  9.2 0.0 copy-start.9
  9.2 0.8 copy-done.9
  10.0 0.0 copy-start.10
  10.0 0.8 copy-done.10
  10.8 0.0 copy-start.12
  10.8 0.7 copy-done.12
  11.5 0.0 copy-start.13
  11.5 0.7 copy-done.13
  12.1 72.2 %shard_map.118 = (f32[4,24,48,192]{3,2,1,0:T(8,128)S(1)}, f32[10,128]{1,0:T(8,128)S(1)}) custom-call(s32[4]{0:T(128)S(1)} %copy-done.13, f32[4,24,48,192]{3,2,1,0:T(8,128)S(1)} %copy-done, f32[24,48,192]{2,1,0:T(8,128)S(1)} %copy-done.2, bf16[2,192,96]{2,1,0:T(8,128)(2,1)S(1)} %copy-done.8, bf16[2,192,192]{2,1,0:T(8,128)(2,1)S(1)} %copy-done.6, ...), custom_call_target="tpu_custom_call" | custom-call | flops 1019215872 | bytes 10485760 | tf_op jit(solution)/shard_map/pallas_call | solution.py:384
  84.4 0.0 copy-start.1
  84.4 2.1 %copy-done.1 = f32[4,24,48,192]{3,2,1,0:T(8,128)} copy-done((f32[4,24,48,192]{3,2,1,0:T(8,128)}, f32[4,24,48,192]{3,2,1,0:T(8,128)S(1)}, u32[]{:S(2)}) %copy-start.1) | copy-done | bytes 3538968
  86.5 0.0 copy-start.11
  86.5 0.6 copy-done.11
  87.1 5.6 %shard_map.119 = f32[4,24,48,192]{3,2,1,0:T(8,128)} custom-call(f32[10,128]{1,0:T(8,128)} %copy-done.11, f32[4,24,48,192]{3,2,1,0:T(8,128)} %copy-done.1), custom_call_target="tpu_custom_call" | custom-call | flops 17694720 | bytes 7077888 | tf_op jit(solution)/shard_map/pallas_call | solution.py:397
Async XLA Ops:
  0.0 2.3 %copy-start = (f32[4,24,48,192]{3,2,1,0:T(8,128)S(1)}, f32[4,24,48,192]{3,2,1,0:T(8,128)}, u32[]{:S(2)}) copy-start(f32[4,24,48,192]{3,2,1,0:T(8,128)} %given.1) | copy-start | bytes 10616836
  2.3 1.3 %copy-start.2 = (f32[24,48,192]{2,1,0:T(8,128)S(1)}, f32[24,48,192]{2,1,0:T(8,128)}, u32[]{:S(2)}) copy-start(f32[24,48,192]{2,1,0:T(8,128)} %given_potential.1) | copy-start | bytes 2654212
  3.6 1.0 %copy-start.3 = (bf16[2,384,192]{2,1,0:T(8,128)(2,1)S(1)}, bf16[2,384,192]{2,1,0:T(8,128)(2,1)}, u32[]{:S(2)}) copy-start(bf16[2,384,192]{2,1,0:T(8,128)(2,1)} %constant.20.clone.fc) | copy-start | bytes 884740
  4.6 1.0 %copy-start.4 = (bf16[2,192,384]{2,1,0:T(8,128)(2,1)S(1)}, bf16[2,192,384]{2,1,0:T(8,128)(2,1)}, u32[]{:S(2)}) copy-start(bf16[2,192,384]{2,1,0:T(8,128)(2,1)} %constant.21.clone.ic) | copy-start | bytes 884740
  5.6 0.9 copy-start.5
  6.5 0.9 copy-start.6
  7.4 0.9 copy-start.7
  8.3 0.9 copy-start.8
  9.2 0.8 copy-start.9
  10.0 0.8 copy-start.10
  10.8 0.7 copy-start.12
  11.5 0.7 copy-start.13
  84.4 2.1 %copy-start.1 = (f32[4,24,48,192]{3,2,1,0:T(8,128)}, f32[4,24,48,192]{3,2,1,0:T(8,128)S(1)}, u32[]{:S(2)}) copy-start(f32[4,24,48,192]{3,2,1,0:T(8,128)S(1)} %get-tuple-element.8.filtered) | copy-start | bytes 10616836
  86.5 0.6 copy-start.11

commit v8 on v7

--- a/solution.py
+++ b/solution.py
@@ -69,9 +69,11 @@
     return product(high, table[0]) + (product(low, table[0]) + product(high, table[1]))
 
 
-def kernel(sizes, unlocked, given, given_potential, fx, fa, fc, ic, ia, ix, row_k, row_f, col_s, kept, solver,
-           orbitals, potential, out, load, store, lines, s1, r1, s2, r2, s3, r3, s4, r4, back, sums, g1, h1, g2, h2,
-           own, send1, recv1, send2, recv2, send3, recv3, send4, recv4, gs1, gr1, gs2, gr2):
+def kernel(sizes, unlocked, given, given_potential, *rest):
+    given_tables, (kept, solver), tables, rest = rest[:9], rest[9:11], rest[11:20], rest[20:]
+    fx, fa, fc, ic, ia, ix, row_k, row_f, col_s = tables
+    (orbitals, potential, out, load, store, load_tables, lines, s1, r1, s2, r2, s3, r3, s4, r4, back, sums, g1, h1, g2, h2,
+           own, send1, recv1, send2, recv2, send3, recv3, send4, recv4, gs1, gr1, gs2, gr2) = rest
     slabs, pencils, chunks, pair, bands, length = sizes
     few = bands // 2
     rows_a = orbitals.shape[1]
@@ -95,10 +97,15 @@
         at = (pl.ds(h * few, few), pl.ds(pl.multiple_of(g * group, group), group))
         return pltpu.make_async_copy(given.at[at], orbitals.at[at], load.at[h, g])
 
+    fetch_tables = [pltpu.make_async_copy(src, dst, load_tables.at[n])
+                    for n, (src, dst) in enumerate(zip(given_tables, tables))]
+    fetch_tables[0].start()
     fetch_potential = pltpu.make_async_copy(given_potential, potential, load.at[2, 0])
     for h in range(2):
         for g in range(rows_a // group):
             fetch(h, g).start()
+    for copy in fetch_tables[1:]:
+        copy.start()
     fetch_potential.start()
 
     def keep(h):
@@ -255,11 +262,14 @@
         lax.fori_loop(first, end, body, 0)
 
     sums[...] = jnp.zeros_like(sums)
+    fetch_tables[0].wait()
     forward_x(0)
     pl.semaphore_wait(barrier, slabs - 1 + pencils - 1)
     for q in range(chunks):
         send_lines(0, q)
     forward_x(1)
+    for copy in fetch_tables[1:]:
+        copy.wait()
     last = 2 * chunks
     for step in range(last + 1):
         if step < last:
@@ -350,12 +360,14 @@
     vmem = pl.BlockSpec(memory_space=pltpu.VMEM)
     f32 = jnp.float32
     dma = pltpu.SemaphoreType.DMA
-    scratch = [
+    given = tables + [row_k, row_f, col_s]
+    scratch = [pltpu.VMEM(t.shape, t.dtype) for t in given] + [
         pltpu.VMEM(orbitals.shape, f32),
         pltpu.VMEM(potential.shape, f32),
         pltpu.VMEM(orbitals.shape, f32),
         dma((3, rows_a // 8)),
         dma((2,)),
+        dma((9,)),
         pltpu.VMEM((2, rows_a * 2 * half, 128), f32),
         pltpu.VMEM((parts, slabs, rows_a, packed), f32),
         pltpu.VMEM((parts, length, packed), f32),
@@ -384,14 +396,13 @@
     filtered, solver = pl.pallas_call(
         functools.partial(kernel, (slabs, pencils, chunks, pair, bands, length)),
         out_shape=[jax.ShapeDtypeStruct(orbitals.shape, f32), jax.ShapeDtypeStruct((pairs, 128), f32)],
-        in_specs=[pl.BlockSpec(memory_space=pltpu.SMEM)] + [pl.BlockSpec(memory_space=pltpu.HBM)] * 2 + [vmem] * 9,
+        in_specs=[pl.BlockSpec(memory_space=pltpu.SMEM), anywhere, anywhere] + [anywhere] * 9,
         out_specs=[anywhere, vmem],
         scratch_shapes=scratch,
         compiler_params=pltpu.CompilerParams(
-            collective_id=0, has_side_effects=True, vmem_limit_bytes=36 * 1024 * 1024),
+            collective_id=0, has_side_effects=True, vmem_limit_bytes=56 * 1024 * 1024),
         cost_estimate=pl.CostEstimate(flops=flops, bytes_accessed=10 * 2**20, transcendentals=0),
-    )(unlocked, orbitals, potential, *[jnp.asarray(t) for t in tables],
-      jnp.asarray(row_k), jnp.asarray(row_f), jnp.asarray(col_s))
+    )(unlocked, orbitals, potential, *[jnp.asarray(t) for t in given])
     planes = 8
     block = pl.BlockSpec((bands, planes, rows_c, length), lambda i: (0, i, 0, 0))
     return pl.pallas_call(

time: 93.3 us -> 78.9 us (0.85)
  local copies, waits for them, and re-layouts: 14.8 us -> 0 us
    unnamed x28 -> x0, local copies, waits for them, and re-layouts: 14.8 us -> none
where the time goes in v8:
time: 78.9 us; the launch traced here: 78.7 us
  Pallas kernels  78.7 us (100%)
    pallas_call x1, Pallas kernels, by_kernel(): pl.pallas_call(functools.partial(kernel, (slabs, pencils, chunks, pair, b...  73 us
    pallas_call x1, Pallas kernels, by_kernel(): pl.pallas_call(solve, grid=(rows_a // planes,), out_shape=jax.ShapeDtypeS...  5.66 us

profile of v8, /device:TPU:0, one launch (start us, length us, event | category | flops | bytes accessed | tf_op | source)
XLA Modules:
  0.0 78.7 jit_solution(10633301060250269065)
XLA Ops:
  0.0 73.0 %shard_map.118 = (f32[4,24,48,192]{3,2,1,0:T(8,128)}, f32[10,128]{1,0:T(8,128)}) custom-call(s32[4]{0:T(128)} %unlocked.1, f32[4,24,48,192]{3,2,1,0:T(8,128)} %given.1, f32[24,48,192]{2,1,0:T(8,128)} %given_potential.1, bf16[2,192,96]{2,1,0:T(8,128)(2,1)} %constant.18.clone.rest_0_, bf16[2,192,192]{2,1,0:T(8,128)(2,1)} %constant.19.clone.rest_1_, ...), custom_call_target="tpu_custom_call" | custom-call | flops 1019215872 | bytes 10485760 | tf_op jit(solution)/shard_map/pallas_call | solution.py:396
  73.0 5.7 %shard_map.119 = f32[4,24,48,192]{3,2,1,0:T(8,128)} custom-call(f32[10,128]{1,0:T(8,128)} %get-tuple-element.7.solver, f32[4,24,48,192]{3,2,1,0:T(8,128)} %get-tuple-element.8.filtered), custom_call_target="tpu_custom_call" | custom-call | flops 17694720 | bytes 7077888 | tf_op jit(solution)/shard_map/pallas_call | solution.py:408
